TPU v7x, 32 devices: a whole 2x2x4 slice. The times are simulated.
32 devices in a mesh: ctx: 8 (over z, x), dp: 4 (over y, core).
Axes of the slice: x: 2, y: 2, z: 4, core: 2. Of those that a mesh axis runs over, the one named last changes fastest.
Arguments:
- tokens: bfloat16 [4, 2048, 768], P('dp', 'ctx'), may hold values from -6 to 6
- cotangent: bfloat16 [4, 2048, 768], P('dp', 'ctx'), may hold values from -6 to 6
- w_query: bfloat16 [768, 768], P('dp'), may hold values from -0.21875 to 0.21875
- w_key: bfloat16 [768, 768], P('dp'), may hold values from -0.21875 to 0.21875
- w_value: bfloat16 [768, 768], P('dp'), may hold values from -0.21875 to 0.21875
- attention_output_weight: bfloat16 [768, 768], P('dp'), may hold values from -3.5 to 3.5
- router: bfloat16 [768, 4], P('dp'), may hold values from -0.15917969 to 0.15917969
- norm1_gain: bfloat16 [768], P('dp'), may hold values from 0.5 to 1.5
- norm2_gain: bfloat16 [768], P('dp'), may hold values from 0.5 to 1.5
- attn_bias: bfloat16 [32, 12], P('dp'), may hold values from -4 to 4
- w_in: bfloat16 [4, 768, 3072], P('dp', None, 'ctx'), may hold values from -0.21875 to 0.21875
- w_out: bfloat16 [4, 3072, 768], P('dp', 'ctx'), may hold values from -0.109375 to 0.109375
- routes: int32 [4, 2048, 2], P('dp', 'ctx'), may hold values from 0 to 3, all different within a row; in each aligned block of 256 rows (0 to 255, 256 to 511, ..., all dimensions but the last counted through in order) at most 256 rows name the same one
- buckets: int32 [2048], replicated, may hold values from 0 to 31
Outputs:
- layer_out: bfloat16 [4, 2048, 768], P('dp', 'ctx')
- input_grad: float32 [4, 2048, 768], P('dp', 'ctx')
- grad_w_query: float32 [768, 768], P('dp')
- grad_w_key: float32 [768, 768], P('dp')
- grad_w_value: float32 [768, 768], P('dp')
- grad_w_output: float32 [768, 768], P('dp')
- grad_router: float32 [768, 4], P('dp')
- grad_norm1_gain: float32 [768], P('dp')
- grad_norm2_gain: float32 [768], P('dp')
- grad_attn_bias: float32 [32, 12], P('dp')
- grad_w_in: float32 [4, 768, 3072], P('dp', None, 'ctx')
- grad_w_out: float32 [4, 3072, 768], P('dp', 'ctx')
Inputs may be any that keep to these rules, and one draw needn't show every extreme that they name: `routes`: the 2 experts of a token differ. Among the tokens of one device (aligned blocks of 256 tokens of a sequence), no expert is named more than 256 times, a bound that some block reaches.
All inputs are finite; a program needn't handle non-finite values.
Results may differ from a plain program's by a relative error of at most 0.02.
Values may be sent and summed in bfloat16 or wider, within the bound.
No kernel may reach another device: no remote copies, remote signals or barrier semaphores. Data moves between devices by JAX's collectives and lax.ppermute only.
A program may use at most 128 MiB of HBM per device.

v0:
```python
import jax
import jax.numpy as jnp
from jax import lax
from jax.sharding import PartitionSpec as P

eps_norm = 1e-06
masked_score = -1e30


def from_behind(block, axis, distance):
    devices = range(lax.axis_size(axis))
    route = [((i - distance) % len(devices), i) for i in devices]
    return lax.ppermute(block, axis, route)


def from_behind_2(value, axis, steps):
    count = lax.axis_size(axis)
    first, last = (max(0, -steps), min(count, count - steps))
    return lax.ppermute(value, axis, [(source, source + steps) for source in range(first, last)])


def norm_apply(inputs, gain):
    return inputs * lax.rsqrt(jnp.mean(inputs * inputs, axis=-1, keepdims=True) + eps_norm) * gain


def gelu_tanh(inputs):
    return jax.nn.gelu(inputs, approximate=True)


def spread_bias(per_distance, length):
    head_count = per_distance.shape[0]
    tiled = jnp.broadcast_to(
        per_distance[:, None, :], (head_count, length, 2 * length - 1)
    ).reshape(head_count, -1)
    tiled = jnp.concatenate([tiled, jnp.zeros((head_count, length), jnp.float32)], axis=1)
    tiled = tiled.reshape(head_count, length, 2 * length)
    return tiled[:, :, :length][:, :, ::-1]


def gather_diagonals(tile):
    head_count = tile.shape[0]
    length = tile.shape[1]
    flipped = tile[:, :, ::-1]
    widened = jnp.concatenate([flipped, jnp.zeros_like(flipped)], axis=2).reshape(head_count, -1)
    sheared = widened[:, : length * (2 * length - 1)].reshape(head_count, length, 2 * length - 1)
    return jnp.sum(sheared, axis=1)


def sum_ctx(gradients):
    return (
        lax.psum(gradients[0].astype(jnp.bfloat16), "ctx").astype(jnp.float32),
        lax.psum(gradients[1].astype(jnp.bfloat16), "ctx").astype(jnp.float32),
        lax.psum(gradients[2].astype(jnp.bfloat16), "ctx").astype(jnp.float32),
        lax.psum(gradients[3].astype(jnp.bfloat16), "ctx").astype(jnp.float32),
        lax.psum(gradients[4].astype(jnp.bfloat16), "ctx").astype(jnp.float32),
        lax.psum(gradients[5].astype(jnp.bfloat16), "ctx").astype(jnp.float32),
        lax.psum(gradients[6].astype(jnp.bfloat16), "ctx").astype(jnp.float32),
        lax.psum(gradients[7].astype(jnp.bfloat16), "ctx").astype(jnp.float32),
    )


def scatter_dp(gradients):
    return (
        lax.psum_scatter(
            gradients[0].astype(jnp.bfloat16), "dp", scatter_dimension=0, tiled=True
        ).astype(jnp.float32),
        lax.psum_scatter(
            gradients[1].astype(jnp.bfloat16), "dp", scatter_dimension=0, tiled=True
        ).astype(jnp.float32),
        lax.psum_scatter(
            gradients[2].astype(jnp.bfloat16), "dp", scatter_dimension=0, tiled=True
        ).astype(jnp.float32),
        lax.psum_scatter(
            gradients[3].astype(jnp.bfloat16), "dp", scatter_dimension=0, tiled=True
        ).astype(jnp.float32),
        lax.psum_scatter(
            gradients[4].astype(jnp.bfloat16), "dp", scatter_dimension=0, tiled=True
        ).astype(jnp.float32),
        lax.psum_scatter(
            gradients[5].astype(jnp.bfloat16), "dp", scatter_dimension=0, tiled=True
        ).astype(jnp.float32),
        lax.psum_scatter(
            gradients[6].astype(jnp.bfloat16), "dp", scatter_dimension=0, tiled=True
        ).astype(jnp.float32),
        lax.psum_scatter(
            gradients[7].astype(jnp.bfloat16), "dp", scatter_dimension=0, tiled=True
        ).astype(jnp.float32),
    )


def send_grads(gradients):
    return (
        from_behind(gradients[0].astype(jnp.bfloat16), "ctx", 1).astype(jnp.float32),
        from_behind(gradients[1].astype(jnp.bfloat16), "ctx", 1).astype(jnp.float32),
    )


def rotate_pairs(carried):
    return from_behind_2((carried[0], carried[1]), "ctx", 1)


def body(
    tokens,
    cotangent,
    w_query,
    w_key,
    w_value,
    attention_output_weight,
    router,
    norm1_gain,
    norm2_gain,
    attn_bias,
    w_in,
    w_out,
    routes,
    buckets,
):
    cycle_size = lax.axis_size("ctx")
    own_index = lax.axis_index("ctx")
    groups = lax.axis_size("dp")
    (
        query_weight,
        key_weight,
        value_weight,
        output_weight,
        router_weight,
        gain_first,
        gain_second,
        bias_table,
    ) = (
        lax.all_gather(w_query, "dp", axis=0, tiled=True),
        lax.all_gather(w_key, "dp", axis=0, tiled=True),
        lax.all_gather(w_value, "dp", axis=0, tiled=True),
        lax.all_gather(attention_output_weight, "dp", axis=0, tiled=True),
        lax.all_gather(router, "dp", axis=0, tiled=True),
        lax.all_gather(norm1_gain, "dp", axis=0, tiled=True),
        lax.all_gather(norm2_gain, "dp", axis=0, tiled=True),
        lax.all_gather(attn_bias, "dp", axis=0, tiled=True),
    )
    expert_in, expert_out = (
        lax.all_gather(w_in, "ctx", axis=2, tiled=True),
        lax.all_gather(w_out, "ctx", axis=1, tiled=True),
    )
    length = tokens.shape[1]
    model_width = tokens.shape[2]
    head_count = bias_table.shape[1]
    head_dim = model_width // head_count
    experts_all = router_weight.shape[1]
    local_experts = w_in.shape[0]
    top_count = routes.shape[2]
    capacity = length * top_count * 2 // experts_all
    first_gain = gain_first.astype(jnp.float32)
    second_gain = gain_second.astype(jnp.float32)
    bias_f32 = bias_table.astype(jnp.float32)
    resid_in = tokens[0].astype(jnp.float32)
    normed_input = norm_apply(resid_in, first_gain).astype(jnp.bfloat16)
    queries = jnp.dot(normed_input, query_weight, preferred_element_type=jnp.float32).astype(
        jnp.bfloat16
    )
    key_rows = jnp.dot(normed_input, key_weight, preferred_element_type=jnp.float32).astype(
        jnp.bfloat16
    )
    value_rows = jnp.dot(normed_input, value_weight, preferred_element_type=jnp.float32).astype(
        jnp.bfloat16
    )
    query3 = queries.reshape(length, head_count, head_dim)
    padded_buckets = jnp.concatenate([jnp.zeros((length,), jnp.int32), buckets])
    bucket_range = jnp.arange(bias_table.shape[0], dtype=jnp.int32)
    row_pos = jnp.arange(length, dtype=jnp.int32)

    def window_onehot(source):
        offset = (own_index - source) * length
        window = lax.dynamic_slice_in_dim(padded_buckets, offset + 1, 2 * length - 1)
        return (window[:, None] == bucket_range[None, :]).astype(jnp.float32)

    def block_scores(key_block, source):
        onehot = window_onehot(source)
        per_distance = jnp.dot(onehot, bias_f32, precision=lax.Precision.HIGHEST).T
        products = (
            jnp.einsum(
                "qhd,khd->hqk",
                query3,
                key_block.reshape(length, head_count, head_dim),
                preferred_element_type=jnp.float32,
            )
            * 0.125
        )
        scores = products + spread_bias(per_distance, length)
        allowed = (own_index - source) * length + row_pos[:, None] - row_pos[None, :] >= 0
        return (jnp.where(allowed[None], scores, masked_score), onehot)

    def cycle_pass(payload, running, visit_block, rotate):

        def one_turn(counter, cycle_state):
            carried, accumulated = cycle_state
            source = (own_index - counter) % cycle_size
            accumulated = lax.cond(
                source <= own_index,
                lambda: visit_block(accumulated, carried, source),
                lambda: accumulated,
            )
            return (rotate(carried), accumulated)

        carried, accumulated = lax.fori_loop(0, cycle_size - 1, one_turn, (payload, running))
        source = (own_index - (cycle_size - 1)) % cycle_size
        return lax.cond(
            source <= own_index,
            lambda: visit_block(accumulated, carried, source),
            lambda: accumulated,
        )

    def total_step(running, key_block, source):
        running_max, running_sum = running
        scores, _ = block_scores(key_block, source)
        new_max = jnp.maximum(running_max, jnp.max(scores, axis=-1))
        new_sum = running_sum * jnp.exp(running_max - new_max) + jnp.sum(
            jnp.exp(scores - new_max[..., None]), axis=-1
        )
        return (new_max, new_sum)

    def value_step(accumulated, carried, source):
        key_block, value_block = carried
        scores, _ = block_scores(key_block, source)
        attn_prob = jnp.exp(scores - log_total[..., None]).astype(jnp.bfloat16)
        return accumulated + jnp.einsum(
            "hqk,khd->qhd",
            attn_prob,
            value_block.reshape(length, head_count, head_dim),
            preferred_element_type=jnp.float32,
        )

    start_max = jnp.full((head_count, length), masked_score, jnp.float32)
    start_sum = jnp.zeros((head_count, length), jnp.float32)
    start_context = jnp.zeros((length, head_count, head_dim), jnp.float32)

    def rotate_keys(carried):
        return from_behind_2(carried, "ctx", 1)

    final_max, final_sum = cycle_pass(key_rows, (start_max, start_sum), total_step, rotate_keys)
    log_total = final_max + jnp.log(final_sum)
    context3 = cycle_pass((key_rows, value_rows), start_context, value_step, rotate_pairs)
    context_rows = context3.reshape(length, model_width)
    context_low = context_rows.astype(jnp.bfloat16)
    attention_result = jnp.dot(context_low, output_weight, preferred_element_type=jnp.float32)
    residual = resid_in + attention_result
    second_choice = norm_apply(residual, second_gain).astype(jnp.bfloat16)
    router_logits = jnp.dot(second_choice, router_weight, preferred_element_type=jnp.float32)
    shifted = router_logits - jnp.max(router_logits, axis=-1, keepdims=True)
    exponent = jnp.exp(shifted)
    chances = exponent / jnp.sum(exponent, axis=-1, keepdims=True)
    route_pairs = routes[0]
    expert_range = jnp.arange(experts_all, dtype=jnp.int32)
    select = (route_pairs[:, :, None] == expert_range[None, None, :]).astype(jnp.float32)
    picked = jnp.sum(select * chances[:, None, :], axis=-1)
    total_pick = jnp.sum(picked, axis=-1, keepdims=True)
    gating = picked / total_pick
    flat_pairs = route_pairs.reshape(-1)
    onehot_int = (flat_pairs[:, None] == expert_range[None, :]).astype(jnp.int32)
    slot_index = jnp.sum((jnp.cumsum(onehot_int, axis=0) - onehot_int) * onehot_int, axis=1)
    destination = flat_pairs * capacity + slot_index
    slot_pair = (
        jnp.zeros((experts_all * capacity,), jnp.int32)
        .at[destination]
        .set(jnp.arange(length * top_count, dtype=jnp.int32))
    )
    slot_used = jnp.zeros((experts_all * capacity,), jnp.bool_).at[destination].set(True)
    outgoing = jnp.where(
        slot_used[:, None], second_choice[slot_pair // top_count], jnp.zeros((), jnp.bfloat16)
    )
    outgoing = outgoing.reshape(groups, local_experts, capacity, model_width)
    received = lax.all_to_all(outgoing, "dp", split_axis=0, concat_axis=0, tiled=True)
    preact = jnp.einsum("secd,edf->secf", received, expert_in, preferred_element_type=jnp.float32)
    hidden = gelu_tanh(preact).astype(jnp.bfloat16)
    expert_result = jnp.einsum(
        "secf,efd->secd", hidden, expert_out, preferred_element_type=jnp.float32
    ).astype(jnp.bfloat16)
    returned = lax.all_to_all(expert_result, "dp", split_axis=0, concat_axis=0, tiled=True).reshape(
        experts_all * capacity, model_width
    )
    chosen = returned[destination].astype(jnp.float32).reshape(length, top_count, model_width)
    mixture = jnp.sum(gating[..., None] * chosen, axis=1)
    layer_out = (residual + mixture).astype(jnp.bfloat16)[None]
    upstream = cotangent[0].astype(jnp.float32)
    grad_gating = jnp.sum(upstream[:, None, :] * chosen, axis=-1)
    scaled = (gating[..., None] * upstream[:, None, :]).reshape(length * top_count, model_width)
    grad_outgoing = jnp.where(slot_used[:, None], scaled[slot_pair], 0.0).astype(jnp.bfloat16)
    grad_outgoing = grad_outgoing.reshape(groups, local_experts, capacity, model_width)
    grad_received = lax.all_to_all(grad_outgoing, "dp", split_axis=0, concat_axis=0, tiled=True)
    grad_hidden = jnp.einsum(
        "secd,efd->secf", grad_received, expert_out, preferred_element_type=jnp.float32
    )
    _, gelu_back = jax.vjp(gelu_tanh, preact)
    grad_preact = gelu_back(grad_hidden)[0].astype(jnp.bfloat16)
    grad_expert_out = jnp.einsum(
        "secf,secd->efd", hidden, grad_received, preferred_element_type=jnp.float32
    )
    grad_expert_in = jnp.einsum(
        "secd,secf->edf", received, grad_preact, preferred_element_type=jnp.float32
    )
    grad_rows = jnp.einsum(
        "secf,edf->secd", grad_preact, expert_in, preferred_element_type=jnp.float32
    ).astype(jnp.bfloat16)
    grad_returned = lax.all_to_all(
        grad_rows, "dp", split_axis=0, concat_axis=0, tiled=True
    ).reshape(experts_all * capacity, model_width)
    moe_grad = jnp.sum(
        grad_returned[destination].astype(jnp.float32).reshape(length, top_count, model_width),
        axis=1,
    )
    grad_pick = grad_gating / total_pick - jnp.sum(grad_gating * picked, axis=-1, keepdims=True) / (
        total_pick * total_pick
    )
    grad_chances = jnp.sum(grad_pick[..., None] * select, axis=1)
    grad_logits = (
        chances * (grad_chances - jnp.sum(chances * grad_chances, axis=-1, keepdims=True))
    ).astype(jnp.bfloat16)
    grad_router = jnp.einsum(
        "td,te->de", second_choice, grad_logits, preferred_element_type=jnp.float32
    )
    grad_second = moe_grad + jnp.einsum(
        "te,de->td", grad_logits, router_weight, preferred_element_type=jnp.float32
    )
    _, second_back = jax.vjp(norm_apply, residual, second_gain)
    grad_resid_norm, grad_gain_second = second_back(grad_second)
    grad_residual = upstream + grad_resid_norm
    grad_attn = grad_residual.astype(jnp.bfloat16)
    grad_output_w = jnp.einsum(
        "td,te->de", context_low, grad_attn, preferred_element_type=jnp.float32
    )
    grad_context = jnp.einsum(
        "te,de->td", grad_attn, output_weight, preferred_element_type=jnp.float32
    ).astype(jnp.bfloat16)
    grad_context3 = grad_context.reshape(length, head_count, head_dim)
    row_delta = jnp.sum(grad_context3.astype(jnp.float32) * context3, axis=-1).T

    def back_visit(carried, gradients, local, source):
        key_block, value_block = carried
        grad_key_acc, grad_value_acc = gradients
        grad_query_acc, grad_bias_acc = local
        key3 = key_block.reshape(length, head_count, head_dim)
        value3 = value_block.reshape(length, head_count, head_dim)
        scores, onehot = block_scores(key_block, source)
        attn_prob = jnp.exp(scores - log_total[..., None])
        grad_prob = jnp.einsum(
            "qhd,khd->hqk", grad_context3, value3, preferred_element_type=jnp.float32
        )
        grad_scores = (attn_prob * (grad_prob - row_delta[..., None])).astype(jnp.bfloat16)
        grad_query_acc = (
            grad_query_acc
            + jnp.einsum("hqk,khd->qhd", grad_scores, key3, preferred_element_type=jnp.float32)
            * 0.125
        )
        grad_key_acc = (
            grad_key_acc
            + jnp.einsum(
                "hqk,qhd->khd", grad_scores, query3, preferred_element_type=jnp.float32
            ).reshape(length, model_width)
            * 0.125
        )
        grad_value_acc = grad_value_acc + jnp.einsum(
            "hqk,qhd->khd",
            attn_prob.astype(jnp.bfloat16),
            grad_context3,
            preferred_element_type=jnp.float32,
        ).reshape(length, model_width)
        diagonal_sums = gather_diagonals(grad_scores.astype(jnp.float32))
        grad_bias_acc = grad_bias_acc + jnp.dot(
            onehot.T, diagonal_sums.T, precision=lax.Precision.HIGHEST
        )
        return ((grad_key_acc, grad_value_acc), (grad_query_acc, grad_bias_acc))

    def back_visit_if(carried, gradients, local, counter):
        source = (own_index - counter) % cycle_size
        return lax.cond(
            source <= own_index,
            lambda: back_visit(carried, gradients, local, source),
            lambda: (gradients, local),
        )

    def back_turn(counter, cycle_state):
        carried, gradients, local = cycle_state
        gradients, local = back_visit_if(carried, gradients, local, counter)
        gradients = send_grads(gradients)
        carried = from_behind_2((carried[0], carried[1]), "ctx", 1)
        return (carried, gradients, local)

    zero_rows = jnp.zeros((length, model_width), jnp.float32)
    start_local = (
        jnp.zeros((length, head_count, head_dim), jnp.float32),
        jnp.zeros(bias_table.shape, jnp.float32),
    )
    carried, gradients, local = lax.fori_loop(
        0, cycle_size - 1, back_turn, ((key_rows, value_rows), (zero_rows, zero_rows), start_local)
    )
    gradients, local = back_visit_if(carried, gradients, local, cycle_size - 1)
    gradients = send_grads(gradients)
    grad_query = local[0].reshape(length, model_width).astype(jnp.bfloat16)
    grad_key = gradients[0].astype(jnp.bfloat16)
    grad_value = gradients[1].astype(jnp.bfloat16)
    grad_bias = local[1]
    grad_query_w = jnp.einsum(
        "td,te->de", normed_input, grad_query, preferred_element_type=jnp.float32
    )
    grad_key_w = jnp.einsum("td,te->de", normed_input, grad_key, preferred_element_type=jnp.float32)
    grad_value_w = jnp.einsum(
        "td,te->de", normed_input, grad_value, preferred_element_type=jnp.float32
    )
    grad_normed = jnp.einsum(
        "te,de->td", grad_query, query_weight, preferred_element_type=jnp.float32
    )
    grad_normed = grad_normed + jnp.einsum(
        "te,de->td", grad_key, key_weight, preferred_element_type=jnp.float32
    )
    grad_normed = grad_normed + jnp.einsum(
        "te,de->td", grad_value, value_weight, preferred_element_type=jnp.float32
    )
    _, first_back = jax.vjp(norm_apply, resid_in, first_gain)
    grad_in_norm, grad_gain_first = first_back(grad_normed)
    input_grad = (grad_residual + grad_in_norm)[None]
    dense = (
        grad_query_w,
        grad_key_w,
        grad_value_w,
        grad_output_w,
        grad_router,
        grad_gain_first,
        grad_gain_second,
        grad_bias,
    )
    summed = scatter_dp(sum_ctx(dense))
    grad_w_in, grad_w_out = (
        lax.psum_scatter(
            grad_expert_in.astype(jnp.bfloat16), "ctx", scatter_dimension=2, tiled=True
        ).astype(jnp.float32),
        lax.psum_scatter(
            grad_expert_out.astype(jnp.bfloat16), "ctx", scatter_dimension=1, tiled=True
        ).astype(jnp.float32),
    )
    return (
        layer_out,
        input_grad,
        summed[0],
        summed[1],
        summed[2],
        summed[3],
        summed[4],
        summed[5],
        summed[6],
        summed[7],
        grad_w_in,
        grad_w_out,
    )


def solution(mesh):
    in_specs = (
        P("dp", "ctx", None),
        P("dp", "ctx", None),
        P("dp", None),
        P("dp", None),
        P("dp", None),
        P("dp", None),
        P("dp", None),
        P("dp"),
        P("dp"),
        P("dp", None),
        P("dp", None, "ctx"),
        P("dp", "ctx", None),
        P("dp", "ctx", None),
        P(),
    )
    out_specs = (
        P("dp", "ctx", None),
        P("dp", "ctx", None),
        P("dp", None),
        P("dp", None),
        P("dp", None),
        P("dp", None),
        P("dp", None),
        P("dp"),
        P("dp"),
        P("dp", None),
        P("dp", None, "ctx"),
        P("dp", "ctx", None),
    )
    return jax.shard_map(body, mesh=mesh, in_specs=in_specs, out_specs=out_specs, check_vma=False)
```

profile of v0, /device:TPU:0, one launch (start us, length us, event | category | flops | bytes accessed | tf_op | source)
XLA Modules:
  0.0 2548.7 jit_solution(7800739974171539753)
XLA Ops:
  70.5 273.9 %while.75 = (s32[]{:T(128)}, bf16[256,768]{0,1:T(8,128)(2,1)}, f32[12,256]{1,0:T(8,128)S(1)}, f32[12,256]{1,0:T(8,128)}, s32[]{:T(128)}, /*index=5*/bf16[256,12,...) while((s32[]{:T(128)}, bf16[256,768]{0,1:T(8,128)(2,1)}, ...), condition=%wide.region_6.7_spmd.clone.clone, body=%wide.region_1.6_spmd.clone.clone.sunk | while | flops 107890424 | bytes 79996032 | solution.py:204
  91.5 50.4 %conditional.18 = ((f32[12,256]{1,0:T(8,128)S(1)}, f32[12,256]{1,0:T(8,128)})) conditional(s32[]{:T(128)} %convert_element_type.563, (f32[12,256]{1,0:T(8,128)S(1)}, f32[12,256]{1,0:T(8,128)}) %tuple.264, (s32[]{:T(128)}, s32[]{:T(128)}, s32[256]{0:T(256)S(1)}, s32[256]{0:T(256)S(1)}, bf16[256,768]{0,1:T(8,128)(2,1)}, ...), branch_computations={%region_2.2_spmd, %region_3.5_spmd} | conditional | flops 107890408 | bytes 77635192 | solution.py:197
  164.2 38.5 %collective-permute-start = (bf16[256,768]{0,1:T(8,128)(2,1)}, bf16[256,768]{0,1:T(8,128)(2,1)}, u32[]{:S(2)}, u32[]{:S(2)}) collective-permute-start(bf16[256,768]{0,1:T(8,128)(2,1)} %copy.225), channel_id=1, source_target_pairs={{0,4},{4,8},{8,12},{12,16},{16,20},{20,24},{24,28},{1,5},{5,9},{9,... | collective-permute-start | bytes 1179656 | tf_op jit(solution)/shard_map/while/body/eval_jaxpr/ppermute | solution.py:19
  242.3 37.6 %collective-permute-start = (bf16[256,768]{0,1:T(8,128)(2,1)}, bf16[256,768]{0,1:T(8,128)(2,1)}, u32[]{:S(2)}, u32[]{:S(2)}) collective-permute-start(bf16[256,768]{0,1:T(8,128)(2,1)} %copy.225), channel_id=1, source_target_pairs={{0,4},{4,8},{8,12},{12,16},{16,20},{20,24},{24,28},{1,5},{5,9},{9,... | collective-permute-start | bytes 1179656 | tf_op jit(solution)/shard_map/while/body/eval_jaxpr/ppermute | solution.py:19
  299.2 39.8 %collective-permute-start = (bf16[256,768]{0,1:T(8,128)(2,1)}, bf16[256,768]{0,1:T(8,128)(2,1)}, u32[]{:S(2)}, u32[]{:S(2)}) collective-permute-start(bf16[256,768]{0,1:T(8,128)(2,1)} %copy.225), channel_id=1, source_target_pairs={{0,4},{4,8},{8,12},{12,16},{16,20},{20,24},{24,28},{1,5},{5,9},{9,... | collective-permute-start | bytes 1179656 | tf_op jit(solution)/shard_map/while/body/eval_jaxpr/ppermute | solution.py:19
  347.1 471.7 %while.76 = (s32[]{:T(128)}, bf16[256,768]{0,1:T(8,128)(2,1)}, bf16[256,768]{0,1:T(8,128)(2,1)}, f32[256,12,64]{0,2,1:T(8,128)}, s32[]{:T(128)}, /*index=5*/bf16...) while((s32[]{:T(128)}, bf16[256,768]{0,1:T(8,128)(2,1)}, ...), condition=%wide.region_14.15_spmd.clone.clone, body=%wide.region_11.14_spmd.clone.clone.sunk | while | flops 207957744 | bytes 71640248 | solution.py:204
  356.7 43.2 %collective-permute-start.2 = (bf16[256,768]{0,1:T(8,128)(2,1)}, bf16[256,768]{0,1:T(8,128)(2,1)}, u32[]{:S(2)}, u32[]{:S(2)}) collective-permute-start(bf16[256,768]{0,1:T(8,128)(2,1)} %copy.242), channel_id=1, source_target_pairs={{0,4},{4,8},{8,12},{12,16},{16,20},{20,24},{24,28},{1,5},{5,9},{9,... | collective-permute-start | bytes 1179656 | tf_op jit(solution)/shard_map/while/body/eval_jaxpr/ppermute | solution.py:19
  399.9 45.9 %conditional.19 = (f32[256,12,64]{0,2,1:T(8,128)}) conditional(s32[]{:T(128)} %convert_element_type.564, f32[256,12,64]{0,2,1:T(8,128)} %get-tuple-element.2215, (s32[]{:T(128)}, s32[]{:T(128)}, s32[256]{0:T(256)S(1)}, s32[256]{0:T(256)S(1)}, bf16[256,768]{0,1:T(8,128)(2,1)}, /*index=5*/bf16[256,12,64]{0,2,1:T(8,128)(2,1)S(1)}, s32[2304]{0:T(1024)}, ...), branch_computations={%region_12.12_spmd, %region_13.13_spmd} | conditional | flops 207957728 | bytes 66920072 | solution.py:197
  454.7 41.7 %collective-permute-start.2 = (bf16[256,768]{0,1:T(8,128)(2,1)}, bf16[256,768]{0,1:T(8,128)(2,1)}, u32[]{:S(2)}, u32[]{:S(2)}) collective-permute-start(bf16[256,768]{0,1:T(8,128)(2,1)} %copy.242), channel_id=1, source_target_pairs={{0,4},{4,8},{8,12},{12,16},{16,20},{20,24},{24,28},{1,5},{5,9},{9,... | collective-permute-start | bytes 1179656 | tf_op jit(solution)/shard_map/while/body/eval_jaxpr/ppermute | solution.py:19
  504.2 44.3 %collective-permute-start.1 = (bf16[256,768]{0,1:T(8,128)(2,1)}, bf16[256,768]{0,1:T(8,128)(2,1)}, u32[]{:S(2)}, u32[]{:S(2)}) collective-permute-start(bf16[256,768]{0,1:T(8,128)(2,1)} %copy.241), channel_id=1, source_target_pairs={{0,4},{4,8},{8,12},{12,16},{16,20},{20,24},{24,28},{1,5},{5,9},{9,... | collective-permute-start | bytes 1179656 | tf_op jit(solution)/shard_map/while/body/eval_jaxpr/ppermute | solution.py:19
  550.3 41.2 %collective-permute-start.2 = (bf16[256,768]{0,1:T(8,128)(2,1)}, bf16[256,768]{0,1:T(8,128)(2,1)}, u32[]{:S(2)}, u32[]{:S(2)}) collective-permute-start(bf16[256,768]{0,1:T(8,128)(2,1)} %copy.242), channel_id=1, source_target_pairs={{0,4},{4,8},{8,12},{12,16},{16,20},{20,24},{24,28},{1,5},{5,9},{9,... | collective-permute-start | bytes 1179656 | tf_op jit(solution)/shard_map/while/body/eval_jaxpr/ppermute | solution.py:19
  599.9 48.8 %collective-permute-start.1 = (bf16[256,768]{0,1:T(8,128)(2,1)}, bf16[256,768]{0,1:T(8,128)(2,1)}, u32[]{:S(2)}, u32[]{:S(2)}) collective-permute-start(bf16[256,768]{0,1:T(8,128)(2,1)} %copy.241), channel_id=1, source_target_pairs={{0,4},{4,8},{8,12},{12,16},{16,20},{20,24},{24,28},{1,5},{5,9},{9,... | collective-permute-start | bytes 1179656 | tf_op jit(solution)/shard_map/while/body/eval_jaxpr/ppermute | solution.py:19
  650.5 40.2 %collective-permute-start.2 = (bf16[256,768]{0,1:T(8,128)(2,1)}, bf16[256,768]{0,1:T(8,128)(2,1)}, u32[]{:S(2)}, u32[]{:S(2)}) collective-permute-start(bf16[256,768]{0,1:T(8,128)(2,1)} %copy.242), channel_id=1, source_target_pairs={{0,4},{4,8},{8,12},{12,16},{16,20},{20,24},{24,28},{1,5},{5,9},{9,... | collective-permute-start | bytes 1179656 | tf_op jit(solution)/shard_map/while/body/eval_jaxpr/ppermute | solution.py:19
  723.1 32.5 %collective-permute-start.1 = (bf16[256,768]{0,1:T(8,128)(2,1)}, bf16[256,768]{0,1:T(8,128)(2,1)}, u32[]{:S(2)}, u32[]{:S(2)}) collective-permute-start(bf16[256,768]{0,1:T(8,128)(2,1)} %copy.241), channel_id=1, source_target_pairs={{0,4},{4,8},{8,12},{12,16},{16,20},{20,24},{24,28},{1,5},{5,9},{9,... | collective-permute-start | bytes 1179656 | tf_op jit(solution)/shard_map/while/body/eval_jaxpr/ppermute | solution.py:19
  781.4 31.4 %collective-permute-start.2 = (bf16[256,768]{0,1:T(8,128)(2,1)}, bf16[256,768]{0,1:T(8,128)(2,1)}, u32[]{:S(2)}, u32[]{:S(2)}) collective-permute-start(bf16[256,768]{0,1:T(8,128)(2,1)} %copy.242), channel_id=1, source_target_pairs={{0,4},{4,8},{8,12},{12,16},{16,20},{20,24},{24,28},{1,5},{5,9},{9,... | collective-permute-start | bytes 1179656 | tf_op jit(solution)/shard_map/while/body/eval_jaxpr/ppermute | solution.py:19
  966.8 1056.8 %while.77 = (s32[]{:T(128)}, bf16[256,768]{0,1:T(8,128)(2,1)S(1)}, bf16[256,768]{0,1:T(8,128)(2,1)S(1)}, f32[256,768]{0,1:T(8,128)}, f32[256,768]{0,1:T(8,128)},...) while((s32[]{:T(128)}, bf16[256,768]{0,1:T(8,128)(2,1)S(1)}, ...), condition=%wide.region_39.40_spmd.clone.clone, body=%wide.region_35.39_spmd.clone.clone.sunk | while | flops 518208064 | bytes 224182208 | solution.py:392
  968.7 99.3 %conditional.20 = ((f32[256,768]{0,1:T(8,128)S(1)}, f32[256,768]{0,1:T(8,128)S(1)}, f32[256,12,64]{0,2,1:T(8,128)S(1)}, f32[32,12]{0,1:T(8,128)})) conditional(s32[]{:T(128)} %convert_element_type.565, (f32[256,768]{0,1:T(8,128)S(1)}, f32[256,768]{0,1:T(8,128)S(1)}, f32[256,12,64]{0,2,1:T(8,128)S(1)}, f32[32,12]{0,1:T(8,128)}) %tuple.270, ...), branch_computations={%region_36.36_spmd, %region_37.38_spmd} | conditional | flops 517028416 | bytes 205305984 | solution.py:374
  1080.0 31.2 %collective-permute-start.3 = (bf16[256,768]{0,1:T(8,128)(2,1)}, bf16[256,768]{0,1:T(8,128)(2,1)S(1)}, u32[]{:S(2)}, u32[]{:S(2)}) collective-permute-start(bf16[256,768]{0,1:T(8,128)(2,1)} %copy.258), channel_id=1, source_target_pairs={{0,4},{4,8},{8,12},{12,16},{16,20},{20,24},{24,28},{1,5},{5,9},{9,... | collective-permute-start | bytes 1179656 | tf_op jit(solution)/shard_map/while/body/eval_jaxpr/ppermute | solution.py:19
  1118.1 70.0 %collective-permute-done.6 = bf16[256,768]{0,1:T(8,128)(2,1)S(1)} collective-permute-done((bf16[256,768]{0,1:T(8,128)(2,1)}, bf16[256,768]{0,1:T(8,128)(2,1)S(1)}, u32[]{:S(2)}, u32[]{:S(2)}) %collective-permute-start.6) | collective-permute-done | bytes 393248 | tf_op jit(solution)/shard_map/while/body/eval_jaxpr/ppermute | solution.py:13
  1200.5 37.0 %collective-permute-start.6 = (bf16[256,768]{0,1:T(8,128)(2,1)}, bf16[256,768]{0,1:T(8,128)(2,1)S(1)}, u32[]{:S(2)}, u32[]{:S(2)}) collective-permute-start(bf16[256,768]{0,1:T(8,128)(2,1)} %convert_element_type.568), channel_id=1, source_target_pairs={{28,0},{0,4},{4,8},{8,12},{12,16},{16,20},{20,24},{24,28},{29,1},{... | collective-permute-start | bytes 1179656 | tf_op jit(solution)/shard_map/while/body/eval_jaxpr/ppermute | solution.py:13
  1238.3 24.2 collective-permute-start.5
  1262.4 39.7 %collective-permute-start.3 = (bf16[256,768]{0,1:T(8,128)(2,1)}, bf16[256,768]{0,1:T(8,128)(2,1)S(1)}, u32[]{:S(2)}, u32[]{:S(2)}) collective-permute-start(bf16[256,768]{0,1:T(8,128)(2,1)} %copy.258), channel_id=1, source_target_pairs={{0,4},{4,8},{8,12},{12,16},{16,20},{20,24},{24,28},{1,5},{5,9},{9,... | collective-permute-start | bytes 1179656 | tf_op jit(solution)/shard_map/while/body/eval_jaxpr/ppermute | solution.py:19
  1339.7 96.6 %collective-permute-start.5 = (bf16[256,768]{0,1:T(8,128)(2,1)}, bf16[256,768]{0,1:T(8,128)(2,1)S(1)}, u32[]{:S(2)}, u32[]{:S(2)}) collective-permute-start(bf16[256,768]{0,1:T(8,128)(2,1)} %convert_element_type.566), channel_id=1, source_target_pairs={{28,0},{0,4},{4,8},{8,12},{12,16},{16,20},{20,24},{24,28},{29,1},{... | collective-permute-start | bytes 1179656 | tf_op jit(solution)/shard_map/while/body/eval_jaxpr/ppermute | solution.py:13
  1478.9 108.0 %collective-permute-start.3 = (bf16[256,768]{0,1:T(8,128)(2,1)}, bf16[256,768]{0,1:T(8,128)(2,1)S(1)}, u32[]{:S(2)}, u32[]{:S(2)}) collective-permute-start(bf16[256,768]{0,1:T(8,128)(2,1)} %copy.258), channel_id=1, source_target_pairs={{0,4},{4,8},{8,12},{12,16},{16,20},{20,24},{24,28},{1,5},{5,9},{9,... | collective-permute-start | bytes 1179656 | tf_op jit(solution)/shard_map/while/body/eval_jaxpr/ppermute | solution.py:19
  1629.8 104.5 %collective-permute-start.4 = (bf16[256,768]{0,1:T(8,128)(2,1)}, bf16[256,768]{0,1:T(8,128)(2,1)S(1)}, u32[]{:S(2)}, u32[]{:S(2)}) collective-permute-start(bf16[256,768]{0,1:T(8,128)(2,1)} %copy.259), channel_id=1, source_target_pairs={{0,4},{4,8},{8,12},{12,16},{16,20},{20,24},{24,28},{1,5},{5,9},{9,... | collective-permute-start | bytes 1179656 | tf_op jit(solution)/shard_map/while/body/eval_jaxpr/ppermute | solution.py:19
  1771.5 103.6 %collective-permute-done.6 = bf16[256,768]{0,1:T(8,128)(2,1)S(1)} collective-permute-done((bf16[256,768]{0,1:T(8,128)(2,1)}, bf16[256,768]{0,1:T(8,128)(2,1)S(1)}, u32[]{:S(2)}, u32[]{:S(2)}) %collective-permute-start.6) | collective-permute-done | bytes 393248 | tf_op jit(solution)/shard_map/while/body/eval_jaxpr/ppermute | solution.py:13
  1907.1 102.7 %collective-permute-done.6 = bf16[256,768]{0,1:T(8,128)(2,1)S(1)} collective-permute-done((bf16[256,768]{0,1:T(8,128)(2,1)}, bf16[256,768]{0,1:T(8,128)(2,1)S(1)}, u32[]{:S(2)}, u32[]{:S(2)}) %collective-permute-start.6) | collective-permute-done | bytes 393248 | tf_op jit(solution)/shard_map/while/body/eval_jaxpr/ppermute | solution.py:13
  2045.0 114.2 %collective-permute-done.8 = bf16[256,768]{0,1:T(8,128)(2,1)S(1)} collective-permute-done((bf16[256,768]{0,1:T(8,128)(2,1)S(1)}, bf16[256,768]{0,1:T(8,128)(2,1)S(1)}, u32[]{:S(2)}, u32[]{:S(2)}) %collective-permute-start.8) | collective-permute-done | bytes 393248 | tf_op jit(solution)/shard_map/ppermute | solution.py:13
  2177.6 28.3 %reduce-scatter.18.cloned.1.call-done = bf16[192,768]{1,0:T(8,128)(2,1)} async-done(((bf16[768,768]{1,0:T(8,128)(2,1)}), bf16[192,768]{1,0:T(8,128)(2,1)}) %reduce-scatter.18.cloned.1.call-update) | async-done | bytes 294928 | tf_op jit(solution)/shard_map/reduce_scatter | solution.py:70
  2205.9 28.9 %reduce-scatter.16.cloned.1.call-done = bf16[192,768]{1,0:T(8,128)(2,1)} async-done(((bf16[768,768]{1,0:T(8,128)(2,1)}), bf16[192,768]{1,0:T(8,128)(2,1)}) %reduce-scatter.16.cloned.1.call-update) | async-done | bytes 294928 | tf_op jit(solution)/shard_map/reduce_scatter | solution.py:67
  2349.7 91.2 %reduce-scatter.22.cloned.1.call-done = bf16[384,768]{1,0:T(8,128)(2,1)} async-done(((bf16[3072,768]{1,0:T(8,128)(2,1)}), bf16[384,768]{1,0:T(8,128)(2,1)}) %reduce-scatter.22.cloned.1.call-update) | async-done | bytes 589840
  2445.3 94.5 %reduce-scatter.12.cloned.1.call-done = bf16[1,384,768]{2,1,0:T(8,128)(2,1)} async-done(((bf16[1,3072,768]{2,1,0:T(8,128)(2,1)}), bf16[1,384,768]{2,1,0:T(8,128)(2,1)}) %reduce-scatter.12.cloned.1.call-update) | async-done | bytes 589840 | tf_op jit(solution)/shard_map/reduce_scatter | solution.py:435
  (619 shorter events, 993.6 us)
Async XLA Ops:
  9.4 820.1 %all-gather.14.cloned.1.call-start = ((), (), s32[]{:S(2)}) async-start(), calls=%async_computation.14 | async-start | bytes 1474560 | tf_op jit(solution)/shard_map/all_gather | solution.py:134
  10.0 864.1 %all-gather.16.cloned.1.call-start = ((), (), s32[]{:S(2)}) async-start(), calls=%async_computation.15 | async-start | bytes 5308416 | tf_op jit(solution)/shard_map/all_gather | solution.py:141
  10.6 873.8 %all-gather.18.cloned.1.call-start = ((), (), s32[]{:S(2)}) async-start(), calls=%async_computation.16 | async-start | bytes 5308416 | tf_op jit(solution)/shard_map/all_gather | solution.py:142
  929.3 1245.5 %reduce-scatter.20.cloned.1.call-start = ((), (), s32[]{:S(2)}) async-start(), calls=%async_computation.21 | async-start | bytes 1474560 | tf_op jit(solution)/shard_map/reduce_scatter | solution.py:73
  966.0 1211.6 %reduce-scatter.14.cloned.1.call-start = ((), (), s32[]{:S(2)}) async-start(), calls=%async_computation.18 | async-start | bytes 1474560 | tf_op jit(solution)/shard_map/reduce_scatter | solution.py:64
  1068.8 119.3 %collective-permute-start.6 = (bf16[256,768]{0,1:T(8,128)(2,1)}, bf16[256,768]{0,1:T(8,128)(2,1)S(1)}, u32[]{:S(2)}, u32[]{:S(2)}) collective-permute-start(bf16[256,768]{0,1:T(8,128)(2,1)} %convert_element_type.568), channel_id=1, source_target_pairs={{28,0},{0,4},{4,8},{8,12},{12,16},{16,20},{20,24},{24,28},{29,1},{... | collective-permute-start | bytes 1179656 | tf_op jit(solution)/shard_map/while/body/eval_jaxpr/ppermute | solution.py:13
  1074.9 120.6 %collective-permute-start.5 = (bf16[256,768]{0,1:T(8,128)(2,1)}, bf16[256,768]{0,1:T(8,128)(2,1)S(1)}, u32[]{:S(2)}, u32[]{:S(2)}) collective-permute-start(bf16[256,768]{0,1:T(8,128)(2,1)} %convert_element_type.566), channel_id=1, source_target_pairs={{28,0},{0,4},{4,8},{8,12},{12,16},{16,20},{20,24},{24,28},{29,1},{... | collective-permute-start | bytes 1179656 | tf_op jit(solution)/shard_map/while/body/eval_jaxpr/ppermute | solution.py:13
  1080.0 116.6 %collective-permute-start.3 = (bf16[256,768]{0,1:T(8,128)(2,1)}, bf16[256,768]{0,1:T(8,128)(2,1)S(1)}, u32[]{:S(2)}, u32[]{:S(2)}) collective-permute-start(bf16[256,768]{0,1:T(8,128)(2,1)} %copy.258), channel_id=1, source_target_pairs={{0,4},{4,8},{8,12},{12,16},{16,20},{20,24},{24,28},{1,5},{5,9},{9,... | collective-permute-start | bytes 1179656 | tf_op jit(solution)/shard_map/while/body/eval_jaxpr/ppermute | solution.py:19
  1200.5 127.0 %collective-permute-start.6 = (bf16[256,768]{0,1:T(8,128)(2,1)}, bf16[256,768]{0,1:T(8,128)(2,1)S(1)}, u32[]{:S(2)}, u32[]{:S(2)}) collective-permute-start(bf16[256,768]{0,1:T(8,128)(2,1)} %convert_element_type.568), channel_id=1, source_target_pairs={{28,0},{0,4},{4,8},{8,12},{12,16},{16,20},{20,24},{24,28},{29,1},{... | collective-permute-start | bytes 1179656 | tf_op jit(solution)/shard_map/while/body/eval_jaxpr/ppermute | solution.py:13
  1338.9 127.0 %collective-permute-start.6 = (bf16[256,768]{0,1:T(8,128)(2,1)}, bf16[256,768]{0,1:T(8,128)(2,1)S(1)}, u32[]{:S(2)}, u32[]{:S(2)}) collective-permute-start(bf16[256,768]{0,1:T(8,128)(2,1)} %convert_element_type.568), channel_id=1, source_target_pairs={{28,0},{0,4},{4,8},{8,12},{12,16},{16,20},{20,24},{24,28},{29,1},{... | collective-permute-start | bytes 1179656 | tf_op jit(solution)/shard_map/while/body/eval_jaxpr/ppermute | solution.py:13
  1339.7 131.8 %collective-permute-start.5 = (bf16[256,768]{0,1:T(8,128)(2,1)}, bf16[256,768]{0,1:T(8,128)(2,1)S(1)}, u32[]{:S(2)}, u32[]{:S(2)}) collective-permute-start(bf16[256,768]{0,1:T(8,128)(2,1)} %convert_element_type.566), channel_id=1, source_target_pairs={{28,0},{0,4},{4,8},{8,12},{12,16},{16,20},{20,24},{24,28},{29,1},{... | collective-permute-start | bytes 1179656 | tf_op jit(solution)/shard_map/while/body/eval_jaxpr/ppermute | solution.py:13
  1476.4 127.0 %collective-permute-start.6 = (bf16[256,768]{0,1:T(8,128)(2,1)}, bf16[256,768]{0,1:T(8,128)(2,1)S(1)}, u32[]{:S(2)}, u32[]{:S(2)}) collective-permute-start(bf16[256,768]{0,1:T(8,128)(2,1)} %convert_element_type.568), channel_id=1, source_target_pairs={{28,0},{0,4},{4,8},{8,12},{12,16},{16,20},{20,24},{24,28},{29,1},{... | collective-permute-start | bytes 1179656 | tf_op jit(solution)/shard_map/while/body/eval_jaxpr/ppermute | solution.py:13
  1477.2 130.8 %collective-permute-start.5 = (bf16[256,768]{0,1:T(8,128)(2,1)}, bf16[256,768]{0,1:T(8,128)(2,1)S(1)}, u32[]{:S(2)}, u32[]{:S(2)}) collective-permute-start(bf16[256,768]{0,1:T(8,128)(2,1)} %convert_element_type.566), channel_id=1, source_target_pairs={{28,0},{0,4},{4,8},{8,12},{12,16},{16,20},{20,24},{24,28},{29,1},{... | collective-permute-start | bytes 1179656 | tf_op jit(solution)/shard_map/while/body/eval_jaxpr/ppermute | solution.py:13
  1478.9 130.1 %collective-permute-start.3 = (bf16[256,768]{0,1:T(8,128)(2,1)}, bf16[256,768]{0,1:T(8,128)(2,1)S(1)}, u32[]{:S(2)}, u32[]{:S(2)}) collective-permute-start(bf16[256,768]{0,1:T(8,128)(2,1)} %copy.258), channel_id=1, source_target_pairs={{0,4},{4,8},{8,12},{12,16},{16,20},{20,24},{24,28},{1,5},{5,9},{9,... | collective-permute-start | bytes 1179656 | tf_op jit(solution)/shard_map/while/body/eval_jaxpr/ppermute | solution.py:19
  1613.0 126.5 %collective-permute-start.6 = (bf16[256,768]{0,1:T(8,128)(2,1)}, bf16[256,768]{0,1:T(8,128)(2,1)S(1)}, u32[]{:S(2)}, u32[]{:S(2)}) collective-permute-start(bf16[256,768]{0,1:T(8,128)(2,1)} %convert_element_type.568), channel_id=1, source_target_pairs={{28,0},{0,4},{4,8},{8,12},{12,16},{16,20},{20,24},{24,28},{29,1},{... | collective-permute-start | bytes 1179656 | tf_op jit(solution)/shard_map/while/body/eval_jaxpr/ppermute | solution.py:13
  1613.8 129.9 %collective-permute-start.5 = (bf16[256,768]{0,1:T(8,128)(2,1)}, bf16[256,768]{0,1:T(8,128)(2,1)S(1)}, u32[]{:S(2)}, u32[]{:S(2)}) collective-permute-start(bf16[256,768]{0,1:T(8,128)(2,1)} %convert_element_type.566), channel_id=1, source_target_pairs={{28,0},{0,4},{4,8},{8,12},{12,16},{16,20},{20,24},{24,28},{29,1},{... | collective-permute-start | bytes 1179656 | tf_op jit(solution)/shard_map/while/body/eval_jaxpr/ppermute | solution.py:13
  1620.0 124.7 %collective-permute-start.3 = (bf16[256,768]{0,1:T(8,128)(2,1)}, bf16[256,768]{0,1:T(8,128)(2,1)S(1)}, u32[]{:S(2)}, u32[]{:S(2)}) collective-permute-start(bf16[256,768]{0,1:T(8,128)(2,1)} %copy.258), channel_id=1, source_target_pairs={{0,4},{4,8},{8,12},{12,16},{16,20},{20,24},{24,28},{1,5},{5,9},{9,... | collective-permute-start | bytes 1179656 | tf_op jit(solution)/shard_map/while/body/eval_jaxpr/ppermute | solution.py:19
  1629.8 114.9 %collective-permute-start.4 = (bf16[256,768]{0,1:T(8,128)(2,1)}, bf16[256,768]{0,1:T(8,128)(2,1)S(1)}, u32[]{:S(2)}, u32[]{:S(2)}) collective-permute-start(bf16[256,768]{0,1:T(8,128)(2,1)} %copy.259), channel_id=1, source_target_pairs={{0,4},{4,8},{8,12},{12,16},{16,20},{20,24},{24,28},{1,5},{5,9},{9,... | collective-permute-start | bytes 1179656 | tf_op jit(solution)/shard_map/while/body/eval_jaxpr/ppermute | solution.py:19
  1748.6 126.5 %collective-permute-start.6 = (bf16[256,768]{0,1:T(8,128)(2,1)}, bf16[256,768]{0,1:T(8,128)(2,1)S(1)}, u32[]{:S(2)}, u32[]{:S(2)}) collective-permute-start(bf16[256,768]{0,1:T(8,128)(2,1)} %convert_element_type.568), channel_id=1, source_target_pairs={{28,0},{0,4},{4,8},{8,12},{12,16},{16,20},{20,24},{24,28},{29,1},{... | collective-permute-start | bytes 1179656 | tf_op jit(solution)/shard_map/while/body/eval_jaxpr/ppermute | solution.py:13
  1750.3 129.0 %collective-permute-start.5 = (bf16[256,768]{0,1:T(8,128)(2,1)}, bf16[256,768]{0,1:T(8,128)(2,1)S(1)}, u32[]{:S(2)}, u32[]{:S(2)}) collective-permute-start(bf16[256,768]{0,1:T(8,128)(2,1)} %convert_element_type.566), channel_id=1, source_target_pairs={{28,0},{0,4},{4,8},{8,12},{12,16},{16,20},{20,24},{24,28},{29,1},{... | collective-permute-start | bytes 1179656 | tf_op jit(solution)/shard_map/while/body/eval_jaxpr/ppermute | solution.py:13
  1757.1 123.2 %collective-permute-start.3 = (bf16[256,768]{0,1:T(8,128)(2,1)}, bf16[256,768]{0,1:T(8,128)(2,1)S(1)}, u32[]{:S(2)}, u32[]{:S(2)}) collective-permute-start(bf16[256,768]{0,1:T(8,128)(2,1)} %copy.258), channel_id=1, source_target_pairs={{0,4},{4,8},{8,12},{12,16},{16,20},{20,24},{24,28},{1,5},{5,9},{9,... | collective-permute-start | bytes 1179656 | tf_op jit(solution)/shard_map/while/body/eval_jaxpr/ppermute | solution.py:19
  1766.4 114.0 %collective-permute-start.4 = (bf16[256,768]{0,1:T(8,128)(2,1)}, bf16[256,768]{0,1:T(8,128)(2,1)S(1)}, u32[]{:S(2)}, u32[]{:S(2)}) collective-permute-start(bf16[256,768]{0,1:T(8,128)(2,1)} %copy.259), channel_id=1, source_target_pairs={{0,4},{4,8},{8,12},{12,16},{16,20},{20,24},{24,28},{1,5},{5,9},{9,... | collective-permute-start | bytes 1179656 | tf_op jit(solution)/shard_map/while/body/eval_jaxpr/ppermute | solution.py:19
  1884.3 125.6 %collective-permute-start.6 = (bf16[256,768]{0,1:T(8,128)(2,1)}, bf16[256,768]{0,1:T(8,128)(2,1)S(1)}, u32[]{:S(2)}, u32[]{:S(2)}) collective-permute-start(bf16[256,768]{0,1:T(8,128)(2,1)} %convert_element_type.568), channel_id=1, source_target_pairs={{28,0},{0,4},{4,8},{8,12},{12,16},{16,20},{20,24},{24,28},{29,1},{... | collective-permute-start | bytes 1179656 | tf_op jit(solution)/shard_map/while/body/eval_jaxpr/ppermute | solution.py:13
  1885.1 129.0 %collective-permute-start.5 = (bf16[256,768]{0,1:T(8,128)(2,1)}, bf16[256,768]{0,1:T(8,128)(2,1)S(1)}, u32[]{:S(2)}, u32[]{:S(2)}) collective-permute-start(bf16[256,768]{0,1:T(8,128)(2,1)} %convert_element_type.566), channel_id=1, source_target_pairs={{28,0},{0,4},{4,8},{8,12},{12,16},{16,20},{20,24},{24,28},{29,1},{... | collective-permute-start | bytes 1179656 | tf_op jit(solution)/shard_map/while/body/eval_jaxpr/ppermute | solution.py:13
  1889.3 125.8 %collective-permute-start.3 = (bf16[256,768]{0,1:T(8,128)(2,1)}, bf16[256,768]{0,1:T(8,128)(2,1)S(1)}, u32[]{:S(2)}, u32[]{:S(2)}) collective-permute-start(bf16[256,768]{0,1:T(8,128)(2,1)} %copy.258), channel_id=1, source_target_pairs={{0,4},{4,8},{8,12},{12,16},{16,20},{20,24},{24,28},{1,5},{5,9},{9,... | collective-permute-start | bytes 1179656 | tf_op jit(solution)/shard_map/while/body/eval_jaxpr/ppermute | solution.py:19
  1898.0 117.1 %collective-permute-start.4 = (bf16[256,768]{0,1:T(8,128)(2,1)}, bf16[256,768]{0,1:T(8,128)(2,1)S(1)}, u32[]{:S(2)}, u32[]{:S(2)}) collective-permute-start(bf16[256,768]{0,1:T(8,128)(2,1)} %copy.259), channel_id=1, source_target_pairs={{0,4},{4,8},{8,12},{12,16},{16,20},{20,24},{24,28},{1,5},{5,9},{9,... | collective-permute-start | bytes 1179656 | tf_op jit(solution)/shard_map/while/body/eval_jaxpr/ppermute | solution.py:19
  2044.8 161.1 %reduce-scatter.18.cloned.1.call-start = ((), (), s32[]{:S(2)}) async-start(), calls=%async_computation.20 | async-start | bytes 1474560 | tf_op jit(solution)/shard_map/reduce_scatter | solution.py:70
  2044.9 114.3 %collective-permute-start.8 = (bf16[256,768]{0,1:T(8,128)(2,1)S(1)}, bf16[256,768]{0,1:T(8,128)(2,1)S(1)}, u32[]{:S(2)}, u32[]{:S(2)}) collective-permute-start(bf16[256,768]{0,1:T(8,128)(2,1)S(1)} %convert_element_type.385), channel_id=1, source_target_pairs={{28,0},{0,4},{4,8},{8,12},{12,16},{16,20},{20,24},{24,28},{29,1},{... | collective-permute-start | bytes 1179656 | tf_op jit(solution)/shard_map/ppermute | solution.py:13
  2173.6 115.0 %reduce-scatter.24.cloned.1.call-start = ((), (), s32[]{:S(2)}) async-start(), calls=%async_computation.23 | async-start | bytes 245760
  2174.7 167.7 %all-reduce.20.cloned.1.call-start = ((), (), s32[]{:S(2)}) async-start(), calls=%async_computation.24 | async-start | bytes 2359296 | tf_op jit(solution)/shard_map/psum | solution.py:51
  2234.9 206.0 %reduce-scatter.22.cloned.1.call-start = ((), (), s32[]{:S(2)}) async-start(), calls=%async_computation.22 | async-start | bytes 5308416
  2271.6 268.3 %reduce-scatter.12.cloned.1.call-start = ((), (), s32[]{:S(2)}) async-start(), calls=%async_computation.17 | async-start | bytes 5308416 | tf_op jit(solution)/shard_map/reduce_scatter | solution.py:435
  (122 other events, 3863.8 us)
Sparse Core Ops, SparseCore 0:
  9.6 20.1 all-gather.7
  31.4 17.4 all-gather.9
  50.4 17.4 all-gather.11
  69.3 17.4 all-gather.13
  88.8 89.7 all-gather.15
  180.6 86.7 all-gather.17
  966.2 130.5 reduce-scatter.19
  2044.9 132.6 reduce-scatter.13
  2180.2 25.7 reduce-scatter.17
  2209.1 25.6 reduce-scatter.15
  2237.9 19.7 reduce-scatter.23
  2261.4 80.9 all-reduce.19
  2346.5 94.3 reduce-scatter.21
  2444.8 95.0 reduce-scatter.11
where the time goes:
time: 2590 us; the launch traced here: 2550 us
  starting transfers between devices  1070 us (41%)
  waiting for transfers between devices  842 us (33%)
  local copies, waits for them, and re-layouts  300 us (12%)
  matrix products  109 us (4%)
  other arithmetic  83 us (3%)
  blocking collectives  73.8 us (3%)
  loops' own time  52.3 us (2%)
    ppermute x35, starting transfers between devices, from_behind_2(): lax.ppermute(value, axis, [(source, source + steps) for source in range(f...  872 us
    ppermute x16, waiting for transfers between devices, from_behind(): return lax.ppermute(block, axis, route)  472 us
    ppermute x16, starting transfers between devices, from_behind(): return lax.ppermute(block, axis, route)  188 us
    unnamed x16, waiting for transfers between devices  95 us
    reduce_scatter x1, waiting for transfers between devices, body(): lax.psum_scatter(grad_expert_out.astype(jnp.bfloat16), 'ctx', scatter_dim...  94.5 us
    ppermute x35, waiting for transfers between devices, from_behind_2(): lax.ppermute(value, axis, [(source, source + steps) for source in range(f...  93.4 us
    rev x3, local copies, waits for them, and re-layouts, spread_bias(): return tiled[:, :, :length][:, :, ::-1]  60.1 us
  transfers between devices with their start and end apart: 68, of which 37 were waited for; matrix products, arithmetic and copies ran while one was open for 18% of the time, Pallas kernels for 0%

commit v1 on v0

v1 whole, which is shorter than its diff:
```python
import functools

import jax
import jax.numpy as jnp
from jax import lax
from jax.experimental import pallas as pl
from jax.experimental.pallas import tpu as pltpu
from jax.sharding import PartitionSpec as P

bf16 = jnp.bfloat16
f32 = jnp.float32
eps_norm = 1e-06
masked_score = -1e30
vmem_bytes = 58 * 1024 * 1024


def dot_f32(a, b, contract):
    return lax.dot_general(a, b, (contract, ((), ())), preferred_element_type=f32)


def xor_move(value, axis, mask):
    count = lax.axis_size(axis)
    return lax.ppermute(value, axis, [(i, i ^ mask) for i in range(count)])


def shift_move(value, axis, step):
    count = lax.axis_size(axis)
    return lax.ppermute(value, axis, [(i, (i + step) % count) for i in range(count)])


def dp_offsets(count):
    offsets, mask = [0], count // 2
    while mask:
        offsets = offsets + [o ^ mask for o in offsets]
        mask //= 2
    return offsets


def gather_dp(block):
    count = lax.axis_size("dp")
    held, mask = [block], count // 2
    while mask:
        held = held + [xor_move(item, "dp", mask) for item in held]
        mask //= 2
    return held


def in_order(held, own):
    count = len(held)
    by_offset = [None] * count
    for offset, item in zip(dp_offsets(count), held):
        by_offset[offset] = item
    mask = 1
    while mask < count:
        swap = (own & mask) != 0
        by_offset = [jnp.where(swap, by_offset[o ^ mask], by_offset[o]) for o in range(count)]
        mask *= 2
    return by_offset


def scatter_sum_dp(parts):
    mask = 1
    while len(parts) > 1:
        half = len(parts) // 2
        arrived = [xor_move(item.astype(bf16), "dp", mask) for item in parts[half:]]
        parts = [mine + other.astype(f32) for mine, other in zip(parts[:half], arrived)]
        mask *= 2
    return parts[0]


def scatter_sum_dp_wide(parts):
    mask = 1
    while len(parts) > 1:
        half = len(parts) // 2
        arrived = [xor_move(item, "dp", mask) for item in parts[half:]]
        parts = [mine + other for mine, other in zip(parts[:half], arrived)]
        mask *= 2
    return parts[0]


def gather_ctx(blocks):
    half = lax.axis_size("ctx") // 2
    same = [blocks] + [[shift_move(item, "ctx", 2 * s) for item in blocks] for s in range(1, half)]
    across = [[xor_move(item, "ctx", 1) for item in entry] for entry in same]
    return same, across


def scatter_sum_ctx(same, across):
    half = lax.axis_size("ctx") // 2
    total = None
    order = list(range(1, half)) + [0]
    for s in order:
        arrived = xor_move(across[s].astype(bf16), "ctx", 1)
        joined = same[s].astype(f32) + arrived.astype(f32)
        if s:
            joined = shift_move(joined.astype(bf16), "ctx", -2 * s).astype(f32)
        total = joined if total is None else total + joined
    return total


def bias_kernel(vec_ref, tile_ref):
    heads, length = tile_ref.shape[0], tile_ref.shape[2]
    d = pl.program_id(0)
    start = pl.multiple_of(d * length, length)
    rows = lax.broadcasted_iota(jnp.int32, (8, 2 * length), 0)
    for h in range(heads):
        base = vec_ref[h : h + 1, pl.ds(start, 2 * length)]
        tile = jnp.broadcast_to(base, (8, 2 * length))
        for bit in (1, 2, 4):
            tile = jnp.where((rows & bit) != 0, pltpu.roll(tile, bit, 1), tile)
        size = 8
        while size < length:
            tile = jnp.concatenate([tile, pltpu.roll(tile, size, 1)], axis=0)
            size *= 2
        tile_ref[h, 0] = tile[:, length:].astype(bf16)


def bias_tiles(vec, heads, blocks, length):
    return pl.pallas_call(
        bias_kernel,
        grid=(blocks,),
        in_specs=[pl.BlockSpec(vec.shape, lambda d: (0, 0))],
        out_specs=pl.BlockSpec((heads, 1, length, length), lambda d: (0, d, 0, 0)),
        out_shape=jax.ShapeDtypeStruct((heads, blocks, length, length), bf16),
        compiler_params=pltpu.CompilerParams(vmem_limit_bytes=vmem_bytes),
        name="bias_tiles",
    )(vec)


def qkv_kernel(count, place_ref, gain_ref, weight_ref, *refs):
    token_refs, (normed_ref, out_ref) = refs[:count], refs[count:]
    length = token_refs[0].shape[0]
    third = weight_ref.shape[0] // 3
    for r in range(count):
        start = pl.multiple_of(place_ref[r] * length, length)
        x = token_refs[r][...].astype(f32)
        scale = lax.rsqrt(jnp.mean(x * x, axis=-1, keepdims=True) + eps_norm)
        normed = (x * scale * gain_ref[...]).astype(bf16)
        normed_ref[pl.ds(start, length), :] = normed
        made = dot_f32(weight_ref[...], normed, ((1,), (1,))).astype(bf16)
        out_ref[:third, pl.ds(start, length)] = (made[:third].astype(f32) * 0.125).astype(bf16)
        out_ref[third:, pl.ds(start, length)] = made[third:]


def project(tokens_held, places, gain, weight):
    count = len(tokens_held)
    length, width = tokens_held[0].shape
    vmem = pl.BlockSpec(memory_space=pltpu.VMEM)
    return pl.pallas_call(
        functools.partial(qkv_kernel, count),
        in_specs=[pl.BlockSpec(memory_space=pltpu.SMEM)] + [vmem] * (count + 2),
        out_specs=[vmem, vmem],
        out_shape=[
            jax.ShapeDtypeStruct((count * length, width), bf16),
            jax.ShapeDtypeStruct((weight.shape[0], count * length), bf16),
        ],
        compiler_params=pltpu.CompilerParams(vmem_limit_bytes=vmem_bytes),
        cost_estimate=pl.CostEstimate(
            flops=2 * count * length * width * weight.shape[0],
            bytes_accessed=2 * count * length * (2 * width + weight.shape[0]),
            transcendentals=0,
        ),
        name="project",
    )(places, gain, weight, *tokens_held)


def attend_kernel(heads, groups, splits, own_ref, qkv_ref, bias_ref, low_ref, wide_ref, lse_ref, k3, acc):
    length = bias_ref.shape[2]
    blocks = bias_ref.shape[1]
    dim = k3.shape[2]
    third = heads * dim
    for h in range(heads):

        def turn(c, _):
            start = pl.multiple_of(c * length, length)
            k3[h, pl.ds(start, length), :] = qkv_ref[
                third + h * dim : third + (h + 1) * dim, pl.ds(start, length)
            ].T
            return 0

        lax.fori_loop(0, blocks, turn, 0)
    own = own_ref[0]
    for j in range(groups):
        block = j * splits + own
        q_start = pl.multiple_of(block * length, length)
        acc[...] = jnp.zeros_like(acc)

        def visit(c, state):
            start = pl.multiple_of(c * length, length)
            out = []
            for h in range(heads):
                top, total = state[h]
                q = qkv_ref[h * dim : (h + 1) * dim, pl.ds(q_start, length)]
                s = dot_f32(k3[h, pl.ds(start, length), :], q, ((1,), (0,)))
                s = s + bias_ref[h, block - c].astype(f32)
                new_top = jnp.maximum(top, jnp.max(s, axis=0, keepdims=True))
                p = jnp.exp(s - new_top)
                fade = jnp.exp(top - new_top)
                total = total * fade + jnp.sum(p, axis=0, keepdims=True)
                v = qkv_ref[2 * third + h * dim : 2 * third + (h + 1) * dim, pl.ds(start, length)]
                acc[h] = acc[h] * fade + dot_f32(v, p.astype(bf16), ((1,), (0,)))
                out.append((new_top, total))
            return tuple(out)

        begin = tuple(
            (jnp.full((1, length), masked_score, f32), jnp.zeros((1, length), f32)) for _ in range(heads)
        )
        state = lax.fori_loop(0, block + 1, visit, begin)
        for h in range(heads):
            top, total = state[h]
            context = acc[h] / total
            wide_ref[j, h * dim : (h + 1) * dim, :] = context
            low_ref[j, h * dim : (h + 1) * dim, :] = context.astype(bf16)
            lse_ref[j, h : h + 1, :] = top + jnp.log(total)


def attend(own, qkv, tiles, groups, splits):
    heads, blocks, length, _ = tiles.shape
    third = qkv.shape[0] // 3
    dim = third // heads
    vmem = pl.BlockSpec(memory_space=pltpu.VMEM)
    units = heads * groups * (blocks + 1) // 2
    return pl.pallas_call(
        functools.partial(attend_kernel, heads, groups, splits),
        in_specs=[pl.BlockSpec(memory_space=pltpu.SMEM), vmem, vmem],
        out_specs=[vmem] * 3,
        out_shape=[
            jax.ShapeDtypeStruct((groups, third, length), bf16),
            jax.ShapeDtypeStruct((groups, third, length), f32),
            jax.ShapeDtypeStruct((groups, 8, length), f32),
        ],
        scratch_shapes=[pltpu.VMEM((heads, blocks * length, dim), bf16), pltpu.VMEM((heads, dim, length), f32)],
        compiler_params=pltpu.CompilerParams(vmem_limit_bytes=vmem_bytes),
        cost_estimate=pl.CostEstimate(
            flops=units * length * length * 256 * 4,
            bytes_accessed=10 * 1024 * 1024,
            transcendentals=units * length * length,
        ),
        name="attend",
    )(own, qkv, tiles)


def attend_back_kernel(
    heads, groups, splits, own_ref, qkv_ref, bias_ref, grad_ref, wide_ref, lse_ref,
    out_ref, diag_ref, k3, v3, grad_k, grad_v, grad_q, grad_b,
):
    length = bias_ref.shape[2]
    blocks = bias_ref.shape[1]
    dim = k3.shape[2]
    third = heads * dim
    for h in range(heads):

        def turn(c, _):
            start = pl.multiple_of(c * length, length)
            k3[h, pl.ds(start, length), :] = qkv_ref[
                third + h * dim : third + (h + 1) * dim, pl.ds(start, length)
            ].T
            v3[h, pl.ds(start, length), :] = qkv_ref[
                2 * third + h * dim : 2 * third + (h + 1) * dim, pl.ds(start, length)
            ].T
            grad_b[h, c] = jnp.zeros((length, length), f32)
            return 0

        lax.fori_loop(0, blocks, turn, 0)
    grad_k[...] = jnp.zeros_like(grad_k)
    grad_v[...] = jnp.zeros_like(grad_v)
    out_ref[:third, :] = jnp.zeros((third, blocks * length), bf16)
    own = own_ref[0]
    for j in range(groups):
        block = j * splits + own
        q_start = pl.multiple_of(block * length, length)
        grad_q[...] = jnp.zeros_like(grad_q)
        delta = []
        for h in range(heads):
            rows = slice(h * dim, (h + 1) * dim)
            delta.append(
                jnp.sum(grad_ref[j, rows, :].astype(f32) * wide_ref[j, rows, :], axis=0, keepdims=True)
            )

        def visit(c, state):
            start = pl.multiple_of(c * length, length)
            for h in range(heads):
                rows = slice(h * dim, (h + 1) * dim)
                q = qkv_ref[h * dim : (h + 1) * dim, pl.ds(q_start, length)]
                g = grad_ref[j, rows, :]
                s = dot_f32(k3[h, pl.ds(start, length), :], q, ((1,), (0,)))
                s = s + bias_ref[h, block - c].astype(f32)
                p = jnp.exp(s - lse_ref[j, h : h + 1, :])
                dp = dot_f32(v3[h, pl.ds(start, length), :], g, ((1,), (0,)))
                ds = (p * (dp - state[h])).astype(bf16)
                grad_v[rows, pl.ds(start, length)] += dot_f32(g, p.astype(bf16), ((1,), (1,)))
                grad_k[rows, pl.ds(start, length)] += dot_f32(q, ds, ((1,), (1,)))
                kt = qkv_ref[third + h * dim : third + (h + 1) * dim, pl.ds(start, length)]
                grad_q[rows, :] += dot_f32(kt, ds, ((1,), (0,)))
                grad_b[h, block - c] += ds.astype(f32)
            return state

        lax.fori_loop(0, block + 1, visit, tuple(delta))
        out_ref[:third, pl.ds(q_start, length)] = (grad_q[...] * 0.125).astype(bf16)
    out_ref[third : 2 * third, :] = grad_k[...].astype(bf16)
    out_ref[2 * third :, :] = grad_v[...].astype(bf16)
    row = lax.broadcasted_iota(jnp.int32, (8, 2 * length), 0)

    def diagonals(d, _):
        for h in range(heads):
            tile = grad_b[h, d]
            tile = jnp.concatenate([jnp.zeros_like(tile), tile], axis=1)
            size = length // 2
            while size >= 8:
                tile = tile[:size] + pltpu.roll(tile[size:], 2 * length - size, 1)
                size //= 2
            for bit in (1, 2, 4):
                tile = jnp.where((row & bit) != 0, pltpu.roll(tile, 2 * length - bit, 1), tile)
            diag_ref[d, h : h + 1, :] = jnp.sum(tile, axis=0, keepdims=True)
        return 0

    lax.fori_loop(0, blocks, diagonals, 0)


def attend_back(own, qkv, tiles, grad_context, wide, lse, groups, splits):
    heads, blocks, length, _ = tiles.shape
    third = qkv.shape[0] // 3
    dim = third // heads
    vmem = pl.BlockSpec(memory_space=pltpu.VMEM)
    units = heads * groups * (blocks + 1) // 2
    return pl.pallas_call(
        functools.partial(attend_back_kernel, heads, groups, splits),
        in_specs=[pl.BlockSpec(memory_space=pltpu.SMEM)] + [vmem] * 5,
        out_specs=[vmem] * 2,
        out_shape=[
            jax.ShapeDtypeStruct((3 * third, blocks * length), bf16),
            jax.ShapeDtypeStruct((blocks, 8, 2 * length), f32),
        ],
        scratch_shapes=[
            pltpu.VMEM((heads, blocks * length, dim), bf16),
            pltpu.VMEM((heads, blocks * length, dim), bf16),
            pltpu.VMEM((third, blocks * length), f32),
            pltpu.VMEM((third, blocks * length), f32),
            pltpu.VMEM((third, length), f32),
            pltpu.VMEM((heads, blocks, length, length), f32),
        ],
        compiler_params=pltpu.CompilerParams(vmem_limit_bytes=vmem_bytes),
        cost_estimate=pl.CostEstimate(
            flops=units * length * length * 256 * 10,
            bytes_accessed=20 * 1024 * 1024,
            transcendentals=units * length * length,
        ),
        name="attend_back",
    )(own, qkv, tiles, grad_context, wide, lse)


def expert_kernel(x_ref, g_ref, weight_ref, out_ref, gx_ref, grad_ref, sum_rows, sum_gx, sum_grad):
    step = pl.program_id(0)
    rows = x_ref.shape[0]
    units = weight_ref.shape[1] // 2
    tile = min(rows, 512)
    root = 0.7978845608028654

    @pl.when(step == 0)
    def _():
        sum_rows[...] = jnp.zeros_like(sum_rows)
        sum_gx[...] = jnp.zeros_like(sum_gx)

    first = weight_ref[0, :units, :]
    second = weight_ref[0, units:, :]
    for at in range(0, rows, tile):
        part = slice(at, at + tile)
        x = x_ref[part, :]
        g = g_ref[part, :]
        pre = dot_f32(x, first, ((1,), (1,)))
        back = dot_f32(g, second, ((1,), (1,)))
        square = pre * pre
        bent = jnp.tanh(root * (pre + 0.044715 * pre * square))
        half = 0.5 * (1.0 + bent)
        hidden = (pre * half).astype(bf16)
        slope = half + 0.5 * pre * (1.0 - bent * bent) * (root * (1.0 + 0.134145 * square))
        gp = (back * slope).astype(bf16)
        sum_rows[part, :] += dot_f32(hidden, second, ((1,), (0,)))
        sum_gx[part, :] += dot_f32(gp, first, ((1,), (0,)))
        grad_first = dot_f32(gp, x, ((0,), (0,)))
        grad_second = dot_f32(hidden, g, ((0,), (0,)))
        if at == 0:
            sum_grad[:units, :] = grad_first
            sum_grad[units:, :] = grad_second
        else:
            sum_grad[:units, :] += grad_first
            sum_grad[units:, :] += grad_second
    grad_ref[0] = sum_grad[...].astype(bf16)

    @pl.when(step == pl.num_programs(0) - 1)
    def _():
        out_ref[...] = sum_rows[...].astype(bf16)
        gx_ref[...] = sum_gx[...].astype(bf16)


def run_expert(x, g, weights):
    rows, width = x.shape
    shards, units = weights.shape[0], weights.shape[1] // 2
    row_spec = pl.BlockSpec((rows, width), lambda i: (0, 0))
    shard_spec = pl.BlockSpec((1, 2 * units, width), lambda i: (i, 0, 0))
    return pl.pallas_call(
        expert_kernel,
        grid=(shards,),
        in_specs=[row_spec, row_spec, shard_spec],
        out_specs=[row_spec, row_spec, shard_spec],
        out_shape=[jax.ShapeDtypeStruct((rows, width), bf16)] * 2 + [jax.ShapeDtypeStruct(weights.shape, bf16)],
        scratch_shapes=[pltpu.VMEM((rows, width), f32)] * 2 + [pltpu.VMEM((2 * units, width), f32)],
        compiler_params=pltpu.CompilerParams(vmem_limit_bytes=vmem_bytes),
        cost_estimate=pl.CostEstimate(
            flops=12 * rows * width * units * shards,
            bytes_accessed=8 * rows * width + 8 * shards * width * units,
            transcendentals=rows * units * shards,
        ),
        name="run_expert",
    )(x, g, weights)


def norm_back(x, gain, grad):
    scale = lax.rsqrt(jnp.mean(x * x, axis=-1, keepdims=True) + eps_norm)
    weighted = grad * gain
    inner = jnp.mean(weighted * x, axis=-1, keepdims=True)
    return scale * weighted - x * (scale * scale * scale) * inner, jnp.sum(grad * x * scale, axis=0)


def body(
    tokens, cotangent, w_query, w_key, w_value, attention_output_weight, router, norm1_gain, norm2_gain,
    attn_bias, w_in, w_out, routes, buckets,
):
    n_ctx = lax.axis_size("ctx")
    n_dp = lax.axis_size("dp")
    ctx_at = lax.axis_index("ctx")
    dp_at = lax.axis_index("dp")
    half = n_ctx // 2
    _, length, width = tokens.shape
    all_heads = attn_bias.shape[1]
    bucket_count = attn_bias.shape[0] * n_dp
    experts = router.shape[1]
    groups = 4
    splits = n_ctx // groups
    heads = all_heads // groups
    dim = width // all_heads
    third = heads * dim
    group_at = ctx_at // splits
    split_at = ctx_at % splits
    rows_dp = w_query.shape[0]

    bias_flat = attn_bias.reshape(1, -1)
    small = jnp.concatenate(
        [
            router.T,
            norm1_gain[None],
            norm2_gain[None],
            jnp.pad(bias_flat, ((0, 0), (0, 2 * rows_dp - bias_flat.shape[1]))).reshape(2, rows_dp)
            if bias_flat.shape[1] > rows_dp
            else jnp.pad(bias_flat, ((0, 0), (0, rows_dp - bias_flat.shape[1]))),
        ],
        axis=0,
    )
    small_all = jnp.stack(in_order(gather_dp(small), dp_at))
    router_weight = small_all[:, :experts, :].transpose(1, 0, 2).reshape(experts, width)
    gain_first = small_all[:, experts, :].reshape(1, width).astype(f32)
    gain_second = small_all[:, experts + 1, :].reshape(1, width).astype(f32)
    bias_table = (
        small_all[:, experts + 2 :, :].reshape(n_dp, -1)[:, : bias_flat.shape[1]].reshape(bucket_count, all_heads)
    )

    own_columns = [
        lax.dynamic_slice_in_dim(w, group_at * third, third, axis=1).T for w in (w_query, w_key, w_value)
    ]
    qkv_part = jnp.concatenate(own_columns, axis=0)
    tok_same, tok_across = gather_ctx([tokens[0]])
    tokens_held = [entry[0] for entry in tok_same + tok_across]
    qkv_weight = jnp.concatenate(in_order(gather_dp(qkv_part), dp_at), axis=1)
    output_weight = jnp.concatenate(in_order(gather_dp(attention_output_weight), dp_at), axis=0)
    upstream_rows = jnp.concatenate(gather_dp(cotangent[0]), axis=0)
    routes_rows = jnp.concatenate(gather_dp(routes[0]), axis=0)

    units = w_in.shape[2]
    expert_weights = lax.all_gather(jnp.concatenate([w_in[0].T, w_out[0]], axis=0), "ctx", axis=0)

    onehot = (buckets[:, None] == jnp.arange(bucket_count, dtype=jnp.int32)[None, :]).astype(bf16)
    bias_own = lax.dynamic_slice_in_dim(bias_table, group_at * heads, heads, axis=1)
    per_distance = dot_f32(bias_own, onehot, ((0,), (1,)))
    vec = jnp.concatenate([jnp.full((heads, length), masked_score, f32), per_distance], axis=1)
    vec = jnp.pad(vec, ((0, 8 - heads), (0, 0)))
    tiles = bias_tiles(vec, heads, n_ctx, length)

    z_at, x_at = ctx_at // 2, ctx_at % 2
    places = jnp.stack(
        [((z_at - s) % half) * 2 + x_at for s in range(half)]
        + [((z_at - s) % half) * 2 + (1 - x_at) for s in range(half)]
    ).astype(jnp.int32)
    normed, qkv = project(tokens_held, places, gain_first, qkv_weight)
    own_split = split_at.astype(jnp.int32).reshape(1)
    low, wide, lse = attend(own_split, qkv, tiles, groups, splits)
    index_groups = [[g * splits + b for g in range(groups)] for b in range(splits)]
    context_t = lax.all_to_all(
        low, "ctx", split_axis=0, concat_axis=0, tiled=True, axis_index_groups=index_groups
    ).reshape(width, length)

    resid_in = tokens[0].astype(f32)
    residual = resid_in + dot_f32(context_t, output_weight, ((0,), (0,)))
    scale2 = lax.rsqrt(jnp.mean(residual * residual, axis=-1, keepdims=True) + eps_norm)
    second = (residual * scale2 * gain_second).astype(bf16)
    second_rows = jnp.concatenate(gather_dp(second), axis=0)

    def gate(rows, pairs):
        logits = dot_f32(rows, router_weight, ((1,), (1,)))
        shifted = jnp.exp(logits - jnp.max(logits, axis=-1, keepdims=True))
        chances = shifted / jnp.sum(shifted, axis=-1, keepdims=True)
        named = jnp.arange(experts, dtype=jnp.int32)[None, :]
        select = jnp.zeros(chances.shape, f32)
        for k in range(pairs.shape[1]):
            select = select + (pairs[:, k : k + 1] == named).astype(f32)
        total = jnp.sum(select * chances, axis=-1, keepdims=True)
        return chances, select, total

    chances_r, select_r, total_r = gate(second_rows, routes_rows)
    own_expert = (jnp.arange(experts, dtype=jnp.int32)[None, :] == dp_at).astype(f32)
    gate_own = jnp.sum(own_expert * select_r * chances_r / total_r, axis=-1, keepdims=True)
    upstream_f = upstream_rows.astype(f32)
    grad_rows = (gate_own * upstream_f).astype(bf16)

    chunk = min(n_dp * length, 1024)
    made = [
        run_expert(second_rows[at : at + chunk], grad_rows[at : at + chunk], expert_weights)
        for at in range(0, n_dp * length, chunk)
    ]
    expert_result = jnp.concatenate([m[0] for m in made], axis=0).astype(f32)
    grad_dispatched = jnp.concatenate([m[1] for m in made], axis=0).astype(f32)
    grad_expert = made[0][2]
    if len(made) > 1:
        grad_expert = sum(m[2].astype(f32) for m in made).astype(bf16)
    grad_expert = lax.psum_scatter(grad_expert, "ctx", scatter_dimension=0, tiled=False).astype(f32)
    grad_w_in = grad_expert[:units].T[None]
    grad_w_out = grad_expert[units:][None]
    grad_gate_rows = jnp.sum(upstream_f * expert_result, axis=-1, keepdims=True) * (own_expert * select_r)
    mixed = gate_own * expert_result
    routed = jnp.sum(own_expert * select_r, axis=-1, keepdims=True)
    grad_dispatched = grad_dispatched * routed

    def by_device(rows):
        return [rows[k * length : (k + 1) * length] for k in range(n_dp)]

    moe_grad = scatter_sum_dp(by_device(grad_dispatched))
    grad_gating = scatter_sum_dp_wide(by_device(grad_gate_rows))

    chances, select, total = gate(second, routes[0])
    inner = jnp.sum(select * grad_gating * chances, axis=-1, keepdims=True)
    grad_chances = select * (grad_gating / total - inner / (total * total))
    grad_logits = (chances * (grad_chances - jnp.sum(chances * grad_chances, axis=-1, keepdims=True))).astype(bf16)
    grad_router = dot_f32(grad_logits, second, ((0,), (0,)))
    grad_second = moe_grad + dot_f32(grad_logits, router_weight, ((1,), (0,)))
    grad_norm, grad_gain_second = norm_back(residual, gain_second, grad_second)
    grad_residual = cotangent[0].astype(f32) + grad_norm
    grad_attn = grad_residual.astype(bf16)

    mixed, _ = lax.optimization_barrier((mixed, grad_attn))
    mixture = scatter_sum_dp(by_device(mixed))
    layer_out = (residual + mixture).astype(bf16)[None]

    grad_context_t = dot_f32(output_weight, grad_attn, ((1,), (1,))).astype(bf16)
    grad_context = lax.all_to_all(
        grad_context_t.reshape(groups, third, length),
        "ctx", split_axis=0, concat_axis=0, tiled=True, axis_index_groups=index_groups,
    )
    grad_output_w = dot_f32(context_t, grad_attn, ((1,), (0,))).astype(bf16)
    grad_output_w = lax.all_to_all(
        grad_output_w.reshape(n_dp, rows_dp, width), "dp", split_axis=0, concat_axis=0, tiled=True
    )
    grad_output_w = jnp.sum(grad_output_w.astype(f32), axis=0)
    grad_output_w = grad_output_w + xor_move(grad_output_w.astype(bf16), "ctx", 1).astype(f32)
    pieces = grad_output_w.astype(bf16)
    for s in range(1, half):
        grad_output_w = grad_output_w + shift_move(pieces, "ctx", 2 * s).astype(f32)
    grad_qkv, diag = attend_back(own_split, qkv, tiles, grad_context, wide, lse, groups, splits)

    gw = dot_f32(grad_qkv, normed, ((1,), (0,)))
    grad_gain_first = jnp.sum(gw * qkv_weight.astype(f32), axis=0) / gain_first[0]
    by_distance = diag[:, :heads, length:].transpose(1, 0, 2).reshape(heads, -1)
    nearer = diag[1:, :heads, :length].transpose(1, 0, 2).reshape(heads, -1)
    by_distance = by_distance + jnp.pad(nearer, ((0, 0), (0, length)))
    grad_bias = lax.dot_general(
        onehot.astype(f32), by_distance, (((0,), (1,)), ((), ())), precision=lax.Precision.HIGHEST
    )
    in_group = (jnp.arange(groups) == group_at).astype(f32)
    grad_bias = (in_group[None, :, None] * grad_bias[:, None, :]).reshape(n_dp, -1)
    bias_rows = -(-grad_bias.shape[1] // rows_dp)
    grad_bias = jnp.pad(grad_bias, ((0, 0), (0, bias_rows * rows_dp - grad_bias.shape[1])))
    small_count = experts + 2 + bias_rows
    parts = jnp.concatenate(
        [
            gw.reshape(3 * third, n_dp, rows_dp).transpose(1, 0, 2),
            grad_router.reshape(experts, n_dp, rows_dp).transpose(1, 0, 2),
            grad_gain_first.reshape(n_dp, 1, rows_dp),
            grad_gain_second.reshape(n_dp, 1, rows_dp),
            grad_bias.reshape(n_dp, bias_rows, rows_dp),
            jnp.zeros((n_dp, -small_count % 16, rows_dp), f32),
        ],
        axis=1,
    ).astype(bf16)
    parts = lax.all_to_all(parts, "dp", split_axis=0, concat_axis=0, tiled=True)
    gw = jnp.sum(parts.astype(f32), axis=0)
    mask = 1
    while mask < splits:
        gw = gw + xor_move(gw.astype(bf16), "ctx", mask).astype(f32)
        mask *= 2
    gw = gw.astype(bf16)
    held = [gw] + [shift_move(gw, "ctx", -splits * s) for s in range(1, groups)]
    small_grads = sum(entry[3 * third :].astype(f32) for entry in held)
    dense = [entry[: 3 * third] for entry in held]
    twice = jnp.concatenate(dense + dense, axis=0)
    begin = ((groups - group_at) % groups) * (3 * third)
    ordered = lax.dynamic_slice_in_dim(twice, begin, groups * 3 * third, axis=0)
    ordered = ordered.reshape(groups, 3, third, rows_dp).transpose(1, 3, 0, 2).reshape(3, rows_dp, width).astype(f32)
    grad_router = small_grads[:experts].T
    grad_gain_first = small_grads[experts]
    grad_gain_second = small_grads[experts + 1]
    grad_bias = small_grads[experts + 2 : small_count].reshape(-1)[: bias_flat.shape[1]].reshape(attn_bias.shape)

    partial = dot_f32(grad_qkv, qkv_weight, ((0,), (0,))).astype(bf16)

    def block_of(s, across):
        at = ((z_at - s) % half) * 2 + (1 - x_at if across else x_at)
        return lax.dynamic_slice_in_dim(partial, at * length, length, axis=0)

    grad_normed = scatter_sum_ctx(
        [block_of(s, False) for s in range(half)], [block_of(s, True) for s in range(half)]
    )
    grad_in_norm = norm_back(resid_in, gain_first, grad_normed)[0]
    input_grad = (grad_residual + grad_in_norm)[None]
    return (
        layer_out, input_grad, ordered[0], ordered[1], ordered[2], grad_output_w, grad_router,
        grad_gain_first, grad_gain_second, grad_bias, grad_w_in, grad_w_out,
    )


def solution(mesh):
    in_specs = (
        P("dp", "ctx", None),
        P("dp", "ctx", None),
        P("dp", None),
        P("dp", None),
        P("dp", None),
        P("dp", None),
        P("dp", None),
        P("dp"),
        P("dp"),
        P("dp", None),
        P("dp", None, "ctx"),
        P("dp", "ctx", None),
        P("dp", "ctx", None),
        P(),
    )
    out_specs = (
        P("dp", "ctx", None),
        P("dp", "ctx", None),
        P("dp", None),
        P("dp", None),
        P("dp", None),
        P("dp", None),
        P("dp", None),
        P("dp"),
        P("dp"),
        P("dp", None),
        P("dp", None, "ctx"),
        P("dp", "ctx", None),
    )
    return jax.shard_map(body, mesh=mesh, in_specs=in_specs, out_specs=out_specs, check_vma=False)
```

time: 2590 us -> 543 us (0.21); the launches traced: 2550 us -> 536 us
  starting transfers between devices: 1070 us -> 103 us
  waiting for transfers between devices: 842 us -> 223 us
  local copies, waits for them, and re-layouts: 300 us -> 38.6 us
  Pallas kernels: 0 us -> 104 us
  matrix products: 109 us -> 17.9 us
  blocking collectives: 73.8 us -> 0 us
  loops' own time: 52.3 us -> 0 us
  other arithmetic: 83 us -> 34 us
    ppermute x51 -> x49, starting transfers between devices: 1060 us -> 54 us  [the longest x37 37.9 us: xor_move(): return lax.ppermute(value, axis, [(i, i ^ mask) for i in range(count)])]
    ppermute x51 -> x49, waiting for transfers between devices: 565 us -> 194 us  [the longest x12 103 us: shift_move(): lax.ppermute(value, axis, [(i, (i + step) % count) for i in range(count)])]
    reduce_scatter x5 -> x1, waiting for transfers between devices: 155 us -> 0.01 us  [body(): lax.psum_scatter(grad_expert, 'ctx', scatter_dimension=0, tiled=False)]
    pallas_call x0 -> x5, Pallas kernels: none -> 104 us  [the longest x1 44.8 us: run_expert(): pl.pallas_call(expert_kernel, grid=(shards,), in_specs=[row_spec, row_spe...]
    unnamed x16 -> x2, waiting for transfers between devices: 95 us -> 0.03 us
    dot_general x32 -> x11, matrix products: 109 us -> 17.9 us  [the longest x10 16.9 us: dot_f32(): lax.dot_general(a, b, (contract, ((), ())), preferred_element_type=f32)]
    rev x4 -> x0, local copies, waits for them, and re-layouts: 77.6 us -> none  [the longest x3 60.1 us: spread_bias(): return tiled[:, :, :length][:, :, ::-1]]
    another operation x27 -> x0, loops' own time: 52.3 us -> none  [the longest x8 17.9 us: back_visit_if(): lax.cond(source <= own_index, lambda: back_visit(carried, gradients, loca...]
  transfers between devices with their start and end apart: 68 -> 55, of which waited for: 37 -> 22; matrix products, arithmetic and copies ran while one was open for 18% -> 14% of each run, Pallas kernels for 0% -> 11%
where the time goes in v1:
time: 543 us; the launch traced here: 536 us
  waiting for transfers between devices  223 us (41%)
  Pallas kernels  104 us (19%)
  starting transfers between devices  103 us (19%)
  local copies, waits for them, and re-layouts  38.6 us (7%)
  other arithmetic  34 us (6%)
  matrix products  17.9 us (3%)
  between operations  15.6 us (3%)
    ppermute x12, waiting for transfers between devices, shift_move(): lax.ppermute(value, axis, [(i, (i + step) % count) for i in range(count)])  103 us
    ppermute x37, waiting for transfers between devices, xor_move(): return lax.ppermute(value, axis, [(i, i ^ mask) for i in range(count)])  90.8 us
    pallas_call x1, Pallas kernels, run_expert(): pl.pallas_call(expert_kernel, grid=(shards,), in_specs=[row_spec, row_spe...  44.8 us
    ppermute x37, starting transfers between devices, xor_move(): return lax.ppermute(value, axis, [(i, i ^ mask) for i in range(count)])  37.9 us
    all_to_all x1, starting transfers between devices, body(): lax.all_to_all(low, 'ctx', split_axis=0, concat_axis=0, tiled=True, axis_...  35.5 us
    pallas_call x1, Pallas kernels, attend_back(): pl.pallas_call(functools.partial(attend_back_kernel, heads, groups, split...  25.5 us
    pallas_call x1, Pallas kernels, attend(): pl.pallas_call(functools.partial(attend_kernel, heads, groups, splits), i...  20 us
    dot_general x10, matrix products, dot_f32(): lax.dot_general(a, b, (contract, ((), ())), preferred_element_type=f32)  16.9 us
  transfers between devices with their start and end apart: 55, of which 22 were waited for; matrix products, arithmetic and copies ran while one was open for 14% of the time, Pallas kernels for 11%

profile of v1, /device:TPU:0, one launch (start us, length us, event | category | flops | bytes accessed | tf_op | source)
XLA Modules:
  0.0 535.9 jit_solution(8396388214114698358)
XLA Ops:
  11.0 3.0 collective-permute-start
  25.4 6.7 %bias_tiles.1.bias_ref = bf16[3,8,256,256]{3,2,1,0:T(8,128)(2,1)} custom-call(f32[8,2304]{1,0:T(8,128)} %pad_select_fusion.vec_ref), custom_call_target="tpu_custom_call" | custom-call | tf_op jit(solution)/shard_map/bias_tiles/pallas_call | solution.py:119
  35.4 29.1 %collective-permute-done.7.refs_2_ = bf16[256,768]{1,0:T(8,128)(2,1)S(1)} collective-permute-done((bf16[256,768]{1,0:T(8,128)(2,1)S(1)}, bf16[256,768]{1,0:T(8,128)(2,1)S(1)}, u32[]{:S(2)}, u32[]{:S(2)}) %collective-permute-start.7) | collective-permute-done | bytes 393248 | tf_op jit(solution)/shard_map/ppermute | solution.py:28
  69.6 6.8 %collective-permute-done.10.refs_5_ = bf16[256,768]{1,0:T(8,128)(2,1)S(1)} collective-permute-done((bf16[256,768]{1,0:T(8,128)(2,1)S(1)}, bf16[256,768]{1,0:T(8,128)(2,1)S(1)}, u32[]{:S(2)}, u32[]{:S(2)}) %collective-permute-start.10) | collective-permute-done | bytes 393248 | tf_op jit(solution)/shard_map/ppermute | solution.py:23
  76.4 8.4 %collective-permute-done.11.refs_6_ = bf16[256,768]{1,0:T(8,128)(2,1)S(1)} collective-permute-done((bf16[256,768]{1,0:T(8,128)(2,1)S(1)}, bf16[256,768]{1,0:T(8,128)(2,1)S(1)}, u32[]{:S(2)}, u32[]{:S(2)}) %collective-permute-start.11) | collective-permute-done | bytes 393248 | tf_op jit(solution)/shard_map/ppermute | solution.py:23
  84.8 7.5 %collective-permute-done.12.refs_7_ = bf16[256,768]{1,0:T(8,128)(2,1)S(1)} collective-permute-done((bf16[256,768]{1,0:T(8,128)(2,1)}, bf16[256,768]{1,0:T(8,128)(2,1)S(1)}, u32[]{:S(2)}, u32[]{:S(2)}) %collective-permute-start.12) | collective-permute-done | bytes 393248 | tf_op jit(solution)/shard_map/ppermute | solution.py:23
  93.1 7.2 %project.1 = (bf16[2048,768]{1,0:T(8,128)(2,1)}, bf16[576,2048]{1,0:T(8,128)(2,1)}) custom-call(s32[8]{0:T(128)} %stack.50.place_ref, f32[1,768]{1,0:T(1,128)} %reshape.208.gain_ref, bf16[576,768]{1,0:T(8,128)(2,1)} %pad_maximum_fusion.4.weight_ref, bf16[256,768]{1,0:T(8,128)(2,1)} %bitcast.113, bf16[256,768]{1,0:T(8,128)(2,1)} %copy-done.47, ...), custom_call_target="tpu_custom_call" | custom-call | flops 1811939328 | bytes 8650752 | tf_op jit(solution)/shard_map/project/pallas_call | solution.py:149
  100.3 20.0 %attend.1 = (bf16[4,192,256]{2,1,0:T(8,128)(2,1)}, f32[4,192,256]{2,1,0:T(8,128)}, f32[4,8,256]{2,1,0:T(8,128)}) custom-call(s32[1]{0:T(128)} %bitcast.1.own_ref, bf16[576,2048]{1,0:T(8,128)(2,1)} %get-tuple-element.23.qkv_ref, bf16[3,8,256,256]{3,2,1,0:T(8,128)(2,1)} %bias_tiles.1.bias_ref), custom_call_target="tpu_custom_call" | custom-call | flops 3623878656 | bytes 10485760 | tf_op jit(solution)/shard_map/attend/pallas_call | solution.py:223
  120.3 35.5 %all-to-all-start = ((bf16[4,192,256]{2,1,0:T(8,128)(2,1)}), bf16[4,192,256]{2,1,0:T(8,128)(2,1)S(1)}, u32[]{:S(2)}, u32[]{:S(2)}) async-start(bf16[4,192,256]{2,1,0:T(8,128)(2,1)} %get-tuple-element.24), calls=%async_computation | async-start | bytes 786432 | tf_op jit(solution)/shard_map/all_to_all | solution.py:497
  159.3 15.3 %all-to-all-done = bf16[4,192,256]{2,1,0:T(8,128)(2,1)S(1)} async-done(((bf16[4,192,256]{2,1,0:T(8,128)(2,1)}), bf16[4,192,256]{2,1,0:T(8,128)(2,1)S(1)}, u32[]{:S(2)}, u32[]{:S(2)}) %all-to-all-start) | async-done | bytes 393248 | tf_op jit(solution)/shard_map/all_to_all | solution.py:497
  180.3 6.5 %collective-permute-done.16 = s32[256,2]{0,1:T(2,128)S(1)} collective-permute-done((s32[256,2]{0,1:T(2,128)S(1)}, s32[256,2]{0,1:T(2,128)S(1)}, u32[]{:S(2)}, u32[]{:S(2)}) %collective-permute-start.16) | collective-permute-done | bytes 2080 | tf_op jit(solution)/shard_map/ppermute | solution.py:23
  188.1 4.5 collective-permute-done.22
  197.8 44.8 %run_expert.1 = (bf16[1024,768]{1,0:T(8,128)(2,1)}, bf16[1024,768]{1,0:T(8,128)(2,1)}, bf16[8,768,768]{2,1,0:T(8,128)(2,1)}) custom-call(bf16[1024,768]{1,0:T(8,128)(2,1)} %copy-done.7, bf16[1024,768]{1,0:T(8,128)(2,1)} %fusion.g_ref, bf16[8,768,768]{2,1,0:T(8,128)(2,1)} %bitcast.153), custom_call_target="tpu_custom_call" | custom-call | flops 28991029248 | bytes 25165824 | tf_op jit(solution)/shard_map/run_expert/pallas_call | solution.py:401
  243.7 2.8 fusion.1
  253.3 9.3 %collective-permute-done.27 = bf16[256,768]{1,0:T(8,128)(2,1)S(1)} collective-permute-done((bf16[256,768]{1,0:T(8,128)(2,1)S(1)}, bf16[256,768]{1,0:T(8,128)(2,1)S(1)}, u32[]{:S(2)}, u32[]{:S(2)}) %collective-permute-start.27) | collective-permute-done | bytes 393248 | tf_op jit(solution)/shard_map/ppermute | solution.py:23
  265.7 4.3 all-to-all-start.1
  279.0 13.6 %all-to-all-done.1.grad_ref = bf16[4,192,256]{2,1,0:T(8,128)(2,1)} async-done(((bf16[4,192,256]{2,1,0:T(8,128)(2,1)}), bf16[4,192,256]{2,1,0:T(8,128)(2,1)}, u32[]{:S(2)}, u32[]{:S(2)}) %all-to-all-start.1) | async-done | bytes 393248 | tf_op jit(solution)/shard_map/all_to_all | solution.py:563
  292.6 4.3 all-to-all-start.3
  296.9 25.5 %attend_back.1 = (bf16[576,2048]{1,0:T(8,128)(2,1)}, f32[8,8,512]{2,1,0:T(8,128)}) custom-call(s32[1]{0:T(128)} %bitcast.1.own_ref, bf16[576,2048]{1,0:T(8,128)(2,1)} %get-tuple-element.23.qkv_ref, bf16[3,8,256,256]{3,2,1,0:T(8,128)(2,1)} %bias_tiles.1.bias_ref, bf16[4,192,256]{2,1,0:T(8,128)(2,1)} %all-to-all-done.1.grad_ref, ...), custom_call_target="tpu_custom_call" | custom-call | flops 9059696640 | bytes 20971520 | tf_op jit(solution)/shard_map/attend_back/pallas_call | solution.py:326
  326.1 5.7 %multiply_reduce_fusion = (f32[768]{0:T(1024)S(1)}, bf16[576,768]{1,0:T(8,128)(2,1)}) fusion(bf16[576,768]{1,0:T(8,128)(2,1)} %pad_maximum_fusion.4.weight_ref, bf16[576,2048]{1,0:T(8,128)(2,1)} %get-tuple-element.30, bf16[2048,768]{1,0:T(8,128)(2,1)} %get-tuple-element.31), kind=kOutput, calls=%fused_computation.9 | convolution fusion | flops 1813708032 | bytes 7277568 | tf_op jit(solution)/shard_map/dot_general | solution.py:18
  335.1 4.6 convolution_convert_fusion
  342.6 11.0 %collective-permute-start.34 = (bf16[256,768]{1,0:T(8,128)(2,1)}, bf16[256,768]{1,0:T(8,128)(2,1)}, u32[]{:S(2)}, u32[]{:S(2)}) collective-permute-start(bf16[256,768]{1,0:T(8,128)(2,1)} %get-tuple-element.115), channel_id=1, source_target_pairs={{0,4},{4,0},{8,12},{12,8},{16,20},{20,16},{24,28},{28,24},{1,5},{5... | collective-permute-start | bytes 1179656 | tf_op jit(solution)/shard_map/ppermute | solution.py:23
  356.5 3.4 concatenate.43
  359.9 4.5 all-to-all-start.2
  371.9 11.1 %collective-permute-done.36 = bf16[256,768]{1,0:T(8,128)(2,1)} collective-permute-done((bf16[256,768]{1,0:T(8,128)(2,1)}, bf16[256,768]{1,0:T(8,128)(2,1)}, u32[]{:S(2)}, u32[]{:S(2)}) %collective-permute-start.36) | collective-permute-done | bytes 393248 | tf_op jit(solution)/shard_map/ppermute | solution.py:23
  383.0 8.4 %collective-permute-done.38 = bf16[256,768]{1,0:T(8,128)(2,1)} collective-permute-done((bf16[256,768]{1,0:T(8,128)(2,1)}, bf16[256,768]{1,0:T(8,128)(2,1)}, u32[]{:S(2)}, u32[]{:S(2)}) %collective-permute-start.38) | collective-permute-done | bytes 393248 | tf_op jit(solution)/shard_map/ppermute | solution.py:23
  394.0 3.7 collective-permute-start.35
  398.3 20.4 %collective-permute-done.45 = bf16[192,768]{1,0:T(8,128)(2,1)S(1)} collective-permute-done((bf16[192,768]{1,0:T(8,128)(2,1)S(1)}, bf16[192,768]{1,0:T(8,128)(2,1)S(1)}, u32[]{:S(2)}, u32[]{:S(2)}) %collective-permute-start.45) | collective-permute-done | bytes 294944 | tf_op jit(solution)/shard_map/ppermute | solution.py:23
  421.0 3.9 collective-permute-start.47
  424.9 52.3 %collective-permute-done.37 = bf16[256,768]{1,0:T(8,128)(2,1)S(1)} collective-permute-done((bf16[256,768]{1,0:T(8,128)(2,1)S(1)}, bf16[256,768]{1,0:T(8,128)(2,1)S(1)}, u32[]{:S(2)}, u32[]{:S(2)}) %collective-permute-start.37) | collective-permute-done | bytes 393248 | tf_op jit(solution)/shard_map/ppermute | solution.py:28
  489.0 2.8 collective-permute-done.42
  491.8 19.0 %collective-permute-done.43 = bf16[592,192]{0,1:T(8,128)(2,1)S(1)} collective-permute-done((bf16[592,192]{0,1:T(8,128)(2,1)S(1)}, bf16[592,192]{0,1:T(8,128)(2,1)S(1)}, u32[]{:S(2)}, u32[]{:S(2)}) %collective-permute-start.43) | collective-permute-done | bytes 227360 | tf_op jit(solution)/shard_map/ppermute | solution.py:28
  (315 shorter events, 114.4 us)
Async XLA Ops:
  7.2 190.6 %all-gather.3.cloned.1.call-start = ((), (), s32[]{:S(2)}) async-start(), calls=%async_computation.6 | async-start | bytes 10616832 | tf_op jit(solution)/shard_map/all_gather | solution.py:479
  15.8 16.3 %collective-permute-start.5 = (bf16[576,192]{1,0:T(8,128)(2,1)S(1)}, bf16[576,192]{1,0:T(8,128)(2,1)S(1)}, u32[]{:S(2)}, u32[]{:S(2)}) collective-permute-start(bf16[576,192]{1,0:T(8,128)(2,1)S(1)} %pad_maximum_fusion.5), channel_id=1, source_target_pairs={{0,1},{1,0},{2,3},{3,2},{4,5},{5,4},{6,7},{7,6},{8,9},{9,8},{10,11... | collective-permute-start | bytes 663560 | tf_op jit(solution)/shard_map/ppermute | solution.py:23
  16.3 17.2 %collective-permute-start.6 = (bf16[256,768]{1,0:T(8,128)(2,1)S(1)}, bf16[256,768]{1,0:T(8,128)(2,1)S(1)}, u32[]{:S(2)}, u32[]{:S(2)}) collective-permute-start(bf16[256,768]{1,0:T(8,128)(2,1)S(1)} %bitcast.114), channel_id=1, source_target_pairs={{0,8},{4,12},{8,16},{12,20},{16,24},{20,28},{24,0},{28,4},{1,9},{5... | collective-permute-start | bytes 1179656 | tf_op jit(solution)/shard_map/ppermute | solution.py:28
  19.0 45.5 %collective-permute-start.7 = (bf16[256,768]{1,0:T(8,128)(2,1)S(1)}, bf16[256,768]{1,0:T(8,128)(2,1)S(1)}, u32[]{:S(2)}, u32[]{:S(2)}) collective-permute-start(bf16[256,768]{1,0:T(8,128)(2,1)S(1)} %bitcast.115), channel_id=1, source_target_pairs={{0,16},{4,20},{8,24},{12,28},{16,0},{20,4},{24,8},{28,12},{1,17},{... | collective-permute-start | bytes 1179656 | tf_op jit(solution)/shard_map/ppermute | solution.py:28
  21.5 44.4 %collective-permute-start.8 = (bf16[256,768]{1,0:T(8,128)(2,1)S(1)}, bf16[256,768]{1,0:T(8,128)(2,1)}, u32[]{:S(2)}, u32[]{:S(2)}) collective-permute-start(bf16[256,768]{1,0:T(8,128)(2,1)S(1)} %bitcast.116), channel_id=1, source_target_pairs={{0,24},{4,28},{8,0},{12,4},{16,8},{20,12},{24,16},{28,20},{1,25},{... | collective-permute-start | bytes 1179656 | tf_op jit(solution)/shard_map/ppermute | solution.py:28
  24.7 41.8 %collective-permute-start.4 = (bf16[576,192]{1,0:T(8,128)(2,1)S(1)}, bf16[576,192]{1,0:T(8,128)(2,1)S(1)}, u32[]{:S(2)}, u32[]{:S(2)}) collective-permute-start(bf16[576,192]{1,0:T(8,128)(2,1)S(1)} %collective-permute-done.3), channel_id=1, source_target_pairs={{0,1},{1,0},{2,3},{3,2},{4,5},{5,4},{6,7},{7,6},{8,9},{9,8},{10,11... | collective-permute-start | bytes 663560 | tf_op jit(solution)/shard_map/ppermute | solution.py:23
  32.1 37.5 %collective-permute-start.9 = (bf16[256,768]{1,0:T(8,128)(2,1)S(1)}, bf16[256,768]{1,0:T(8,128)(2,1)S(1)}, u32[]{:S(2)}, u32[]{:S(2)}) collective-permute-start(bf16[256,768]{1,0:T(8,128)(2,1)S(1)} %bitcast.117), channel_id=1, source_target_pairs={{0,4},{4,0},{8,12},{12,8},{16,20},{20,16},{24,28},{28,24},{1,5},{5... | collective-permute-start | bytes 1179656 | tf_op jit(solution)/shard_map/ppermute | solution.py:23
  33.6 122.5 %collective-permute-start.13 = (bf16[192,768]{1,0:T(8,128)(2,1)S(1)}, bf16[192,768]{1,0:T(8,128)(2,1)S(1)}, u32[]{:S(2)}, u32[]{:S(2)}) collective-permute-start(bf16[192,768]{1,0:T(8,128)(2,1)S(1)} %copy-done.29), channel_id=1, source_target_pairs={{0,2},{1,3},{2,0},{3,1},{4,6},{5,7},{6,4},{7,5},{8,10},{9,11},{10,... | collective-permute-start | bytes 884744 | tf_op jit(solution)/shard_map/ppermute | solution.py:23
  65.9 18.9 %collective-permute-start.11 = (bf16[256,768]{1,0:T(8,128)(2,1)S(1)}, bf16[256,768]{1,0:T(8,128)(2,1)S(1)}, u32[]{:S(2)}, u32[]{:S(2)}) collective-permute-start(bf16[256,768]{1,0:T(8,128)(2,1)S(1)} %collective-permute-done.7.refs_2_), channel_id=1, source_target_pairs={{0,4},{4,0},{8,12},{12,8},{16,20},{20,16},{24,28},{28,24},{1,5},{5... | collective-permute-start | bytes 1179656 | tf_op jit(solution)/shard_map/ppermute | solution.py:23
  66.5 25.9 %collective-permute-start.12 = (bf16[256,768]{1,0:T(8,128)(2,1)}, bf16[256,768]{1,0:T(8,128)(2,1)S(1)}, u32[]{:S(2)}, u32[]{:S(2)}) collective-permute-start(bf16[256,768]{1,0:T(8,128)(2,1)} %collective-permute-done.8.refs_3_), channel_id=1, source_target_pairs={{0,4},{4,0},{8,12},{12,8},{16,20},{20,16},{24,28},{28,24},{1,5},{5... | collective-permute-start | bytes 1179656 | tf_op jit(solution)/shard_map/ppermute | solution.py:23
  120.3 54.3 %all-to-all-start = ((bf16[4,192,256]{2,1,0:T(8,128)(2,1)}), bf16[4,192,256]{2,1,0:T(8,128)(2,1)S(1)}, u32[]{:S(2)}, u32[]{:S(2)}) async-start(bf16[4,192,256]{2,1,0:T(8,128)(2,1)} %get-tuple-element.24), calls=%async_computation | async-start | bytes 786432 | tf_op jit(solution)/shard_map/all_to_all | solution.py:497
  155.8 368.8 %reduce-scatter.2.cloned.1.call-start = ((), (), s32[]{:S(2)}) async-start(), calls=%async_computation.5 | async-start | bytes 10616832 | tf_op jit(solution)/shard_map/reduce_scatter | solution.py:534
  178.4 14.2 %collective-permute-start.22 = (bf16[256,768]{1,0:T(8,128)(2,1)S(1)}, bf16[256,768]{1,0:T(8,128)(2,1)S(1)}, u32[]{:S(2)}, u32[]{:S(2)}) collective-permute-start(bf16[256,768]{1,0:T(8,128)(2,1)S(1)} %bitcast.104), channel_id=1, source_target_pairs={{0,2},{1,3},{2,0},{3,1},{4,6},{5,7},{6,4},{7,5},{8,10},{9,11},{10,... | collective-permute-start | bytes 1179656 | tf_op jit(solution)/shard_map/ppermute | solution.py:23
  180.0 15.5 %collective-permute-start.23 = (bf16[256,768]{1,0:T(8,128)(2,1)S(1)}, bf16[256,768]{1,0:T(8,128)(2,1)S(1)}, u32[]{:S(2)}, u32[]{:S(2)}) collective-permute-start(bf16[256,768]{1,0:T(8,128)(2,1)S(1)} %bitcast.105), channel_id=1, source_target_pairs={{0,1},{1,0},{2,3},{3,2},{4,5},{5,4},{6,7},{7,6},{8,9},{9,8},{10,11... | collective-permute-start | bytes 1179656 | tf_op jit(solution)/shard_map/ppermute | solution.py:23
  265.7 26.9 %all-to-all-start.1 = ((bf16[4,192,256]{2,1,0:T(8,128)(2,1)}), bf16[4,192,256]{2,1,0:T(8,128)(2,1)}, u32[]{:S(2)}, u32[]{:S(2)}) async-start(bf16[4,192,256]{2,1,0:T(8,128)(2,1)} %bitcast.134), calls=%async_computation.1 | async-start | bytes 786432 | tf_op jit(solution)/shard_map/all_to_all | solution.py:563
  273.2 92.8 %collective-permute-start.31 = (bf16[256,768]{1,0:T(8,128)(2,1)}, bf16[256,768]{1,0:T(8,128)(2,1)}, u32[]{:S(2)}, u32[]{:S(2)}) collective-permute-start(bf16[256,768]{1,0:T(8,128)(2,1)} %get-tuple-element.126), channel_id=1, source_target_pairs={{0,1},{1,0},{2,3},{3,2},{4,5},{5,4},{6,7},{7,6},{8,9},{9,8},{10,11... | collective-permute-start | bytes 1179656 | tf_op jit(solution)/shard_map/ppermute | solution.py:23
  278.1 88.0 %collective-permute-start.33 = (bf16[256,768]{1,0:T(8,128)(2,1)}, bf16[256,768]{1,0:T(8,128)(2,1)}, u32[]{:S(2)}, u32[]{:S(2)}) collective-permute-start(bf16[256,768]{1,0:T(8,128)(2,1)} %add_convert_fusion.4), channel_id=1, source_target_pairs={{0,2},{1,3},{2,0},{3,1},{4,6},{5,7},{6,4},{7,5},{8,10},{9,11},{10,... | collective-permute-start | bytes 1179656 | tf_op jit(solution)/shard_map/ppermute | solution.py:23
  292.6 67.3 %all-to-all-start.3 = ((bf16[4,192,768]{2,1,0:T(8,128)(2,1)}), bf16[4,192,768]{2,1,0:T(8,128)(2,1)}, u32[]{:S(2)}, u32[]{:S(2)}) async-start(bf16[4,192,768]{2,1,0:T(8,128)(2,1)} %bitcast.101), calls=%async_computation.3 | async-start | bytes 2359296 | tf_op jit(solution)/shard_map/all_to_all | solution.py:568
  342.6 29.3 %collective-permute-start.34 = (bf16[256,768]{1,0:T(8,128)(2,1)}, bf16[256,768]{1,0:T(8,128)(2,1)}, u32[]{:S(2)}, u32[]{:S(2)}) collective-permute-start(bf16[256,768]{1,0:T(8,128)(2,1)} %get-tuple-element.115), channel_id=1, source_target_pairs={{0,4},{4,0},{8,12},{12,8},{16,20},{20,16},{24,28},{28,24},{1,5},{5... | collective-permute-start | bytes 1179656 | tf_op jit(solution)/shard_map/ppermute | solution.py:23
  353.7 29.3 %collective-permute-start.36 = (bf16[256,768]{1,0:T(8,128)(2,1)}, bf16[256,768]{1,0:T(8,128)(2,1)}, u32[]{:S(2)}, u32[]{:S(2)}) collective-permute-start(bf16[256,768]{1,0:T(8,128)(2,1)} %get-tuple-element.118), channel_id=1, source_target_pairs={{0,4},{4,0},{8,12},{12,8},{16,20},{20,16},{24,28},{28,24},{1,5},{5... | collective-permute-start | bytes 1179656 | tf_op jit(solution)/shard_map/ppermute | solution.py:23
  353.7 37.7 %collective-permute-start.38 = (bf16[256,768]{1,0:T(8,128)(2,1)}, bf16[256,768]{1,0:T(8,128)(2,1)}, u32[]{:S(2)}, u32[]{:S(2)}) collective-permute-start(bf16[256,768]{1,0:T(8,128)(2,1)} %get-tuple-element.117), channel_id=1, source_target_pairs={{0,4},{4,0},{8,12},{12,8},{16,20},{20,16},{24,28},{28,24},{1,5},{5... | collective-permute-start | bytes 1179656 | tf_op jit(solution)/shard_map/ppermute | solution.py:23
  359.9 59.6 %all-to-all-start.2 = ((bf16[4,592,192]{1,2,0:T(8,128)(2,1)}), bf16[4,592,192]{1,2,0:T(8,128)(2,1)}, u32[]{:S(2)}, u32[]{:S(2)}) async-start(bf16[4,592,192]{1,2,0:T(8,128)(2,1)} %concatenate.43), calls=%async_computation.2 | async-start | bytes 1966080 | tf_op jit(solution)/shard_map/all_to_all | solution.py:602
  366.0 55.0 %collective-permute-start.40 = (bf16[256,768]{1,0:T(8,128)(2,1)}, bf16[256,768]{1,0:T(8,128)(2,1)}, u32[]{:S(2)}, u32[]{:S(2)}) collective-permute-start(bf16[256,768]{1,0:T(8,128)(2,1)} %get-tuple-element.116), channel_id=1, source_target_pairs={{0,4},{4,0},{8,12},{12,8},{16,20},{20,16},{24,28},{28,24},{1,5},{5... | collective-permute-start | bytes 1179656 | tf_op jit(solution)/shard_map/ppermute | solution.py:23
  366.1 52.5 %collective-permute-start.45 = (bf16[192,768]{1,0:T(8,128)(2,1)S(1)}, bf16[192,768]{1,0:T(8,128)(2,1)S(1)}, u32[]{:S(2)}, u32[]{:S(2)}) collective-permute-start(bf16[192,768]{1,0:T(8,128)(2,1)S(1)} %convert_element_type.288), channel_id=1, source_target_pairs={{0,4},{4,0},{8,12},{12,8},{16,20},{20,16},{24,28},{28,24},{1,5},{5... | collective-permute-start | bytes 884744 | tf_op jit(solution)/shard_map/ppermute | solution.py:23
  394.0 30.9 %collective-permute-start.35 = (bf16[256,768]{1,0:T(8,128)(2,1)}, bf16[256,768]{1,0:T(8,128)(2,1)S(1)}, u32[]{:S(2)}, u32[]{:S(2)}) collective-permute-start(bf16[256,768]{1,0:T(8,128)(2,1)} %get-tuple-element.112), channel_id=1, source_target_pairs={{0,24},{4,28},{8,0},{12,4},{16,8},{20,12},{24,16},{28,20},{1,25},{... | collective-permute-start | bytes 1179656 | tf_op jit(solution)/shard_map/ppermute | solution.py:28
  397.7 79.5 %collective-permute-start.37 = (bf16[256,768]{1,0:T(8,128)(2,1)S(1)}, bf16[256,768]{1,0:T(8,128)(2,1)S(1)}, u32[]{:S(2)}, u32[]{:S(2)}) collective-permute-start(bf16[256,768]{1,0:T(8,128)(2,1)S(1)} %get-tuple-element.114), channel_id=1, source_target_pairs={{0,16},{4,20},{8,24},{12,28},{16,0},{20,4},{24,8},{28,12},{1,17},{... | collective-permute-start | bytes 1179656 | tf_op jit(solution)/shard_map/ppermute | solution.py:28
  397.7 80.9 %collective-permute-start.39 = (bf16[256,768]{1,0:T(8,128)(2,1)S(1)}, bf16[256,768]{1,0:T(8,128)(2,1)S(1)}, u32[]{:S(2)}, u32[]{:S(2)}) collective-permute-start(bf16[256,768]{1,0:T(8,128)(2,1)S(1)} %get-tuple-element.113), channel_id=1, source_target_pairs={{0,8},{4,12},{8,16},{12,20},{16,24},{20,28},{24,0},{28,4},{1,9},{5... | collective-permute-start | bytes 1179656 | tf_op jit(solution)/shard_map/ppermute | solution.py:28
  419.5 65.6 %collective-permute-start.46 = (bf16[192,768]{1,0:T(8,128)(2,1)}, bf16[192,768]{1,0:T(8,128)(2,1)}, u32[]{:S(2)}, u32[]{:S(2)}) collective-permute-start(bf16[192,768]{1,0:T(8,128)(2,1)} %fusion.17), channel_id=1, source_target_pairs={{0,8},{4,12},{8,16},{12,20},{16,24},{20,28},{24,0},{28,4},{1,9},{5... | collective-permute-start | bytes 884744 | tf_op jit(solution)/shard_map/ppermute | solution.py:28
  421.0 66.0 %collective-permute-start.47 = (bf16[192,768]{1,0:T(8,128)(2,1)}, bf16[192,768]{1,0:T(8,128)(2,1)S(1)}, u32[]{:S(2)}, u32[]{:S(2)}) collective-permute-start(bf16[192,768]{1,0:T(8,128)(2,1)} %fusion.17), channel_id=1, source_target_pairs={{0,16},{4,20},{8,24},{12,28},{16,0},{20,4},{24,8},{28,12},{1,17},{... | collective-permute-start | bytes 884744 | tf_op jit(solution)/shard_map/ppermute | solution.py:28
  424.9 62.1 %collective-permute-start.48 = (bf16[192,768]{1,0:T(8,128)(2,1)}, bf16[192,768]{1,0:T(8,128)(2,1)S(1)}, u32[]{:S(2)}, u32[]{:S(2)}) collective-permute-start(bf16[192,768]{1,0:T(8,128)(2,1)} %fusion.17), channel_id=1, source_target_pairs={{0,24},{4,28},{8,0},{12,4},{16,8},{20,12},{24,16},{28,20},{1,25},{... | collective-permute-start | bytes 884744 | tf_op jit(solution)/shard_map/ppermute | solution.py:28
  485.0 25.8 %collective-permute-start.43 = (bf16[592,192]{0,1:T(8,128)(2,1)S(1)}, bf16[592,192]{0,1:T(8,128)(2,1)S(1)}, u32[]{:S(2)}, u32[]{:S(2)}) collective-permute-start(bf16[592,192]{0,1:T(8,128)(2,1)S(1)} %add_convert_fusion.5), channel_id=1, source_target_pairs={{0,16},{4,20},{8,24},{12,28},{16,0},{20,4},{24,8},{28,12},{1,17},{... | collective-permute-start | bytes 681992 | tf_op jit(solution)/shard_map/ppermute | solution.py:28
  485.1 25.7 %collective-permute-start.44 = (bf16[592,192]{0,1:T(8,128)(2,1)S(1)}, bf16[592,192]{0,1:T(8,128)(2,1)S(1)}, u32[]{:S(2)}, u32[]{:S(2)}) collective-permute-start(bf16[592,192]{0,1:T(8,128)(2,1)S(1)} %add_convert_fusion.5), channel_id=1, source_target_pairs={{0,8},{4,12},{8,16},{12,20},{16,24},{20,28},{24,0},{28,4},{1,9},{5... | collective-permute-start | bytes 681992 | tf_op jit(solution)/shard_map/ppermute | solution.py:28
  (80 other events, 1101.7 us)
Sparse Core Ops, SparseCore 0:
  11.0 178.7 all-gather.2
  242.8 235.6 reduce-scatter.1
